TPU v7x, 32 devices: a whole 2x2x4 slice. The times are simulated.
32 devices in a mesh: grp: 2 (over x), chan: 16 (over z, y, core).
Axes of the slice: x: 2, y: 2, z: 4, core: 2. Of those that a mesh axis runs over, the one named last changes fastest.
Arguments:
- voltages: int32 [512, 2, 2, 32, 1024], P(('grp', 'chan')), parts along dimension 0, may hold values from -127 to 127
- scales: int32 [512, 1024], P(('grp', 'chan')), parts along dimension 0, may hold values from 1 to 8
- feed_positions: float32 [3, 1024], replicated, may hold values from -8 to 8
- beam_directions: float32 [3, 128], replicated, may hold values from -1 to 1
- dm_trials: int32 [256], replicated, may hold values from 0 to 255, each once
Outputs:
- dedispersed: float32 [256, 32, 256], P(None, ('grp', 'chan')), parts along dimension 1
There are 2 independent parts, one for each index of `grp`. A program takes and returns all parts, laid end to end along the dimension named above; an argument that names none is the same for every part. Nothing has to cross between parts.
Inputs may be any that keep to these rules, and one draw needn't show every extreme that they name: dm_trials holds each number of 0 to 255 once.
All inputs are finite; a program needn't handle non-finite values.
Results may differ from a plain program's by a relative error of at most 0.0046.
Values may be sent and summed in bfloat16 or wider, within the bound.
No kernel may reach another device: no remote copies, remote signals or barrier semaphores. Data moves between devices by JAX's collectives and lax.ppermute only.
A program may use at most 320 MiB of HBM per device.

v0:
```python
import math

import jax
import jax.numpy as jnp
from jax import lax
from jax.sharding import PartitionSpec as P

MAXD = 15


TWO_PI = 6.283185307179586
POWER_SCALE = 1.0 / 67108864.0


def passed_along(value, axis, steps):
    count = lax.axis_size(axis)
    leading, last = (max(0, -steps), min(count, count - steps))
    return lax.ppermute(value, axis, [(source, source + steps) for source in range(leading, last)])


def geometry_delay(feed_positions, beam_directions):
    total = feed_positions[0][:, None] * beam_directions[0][None, :]
    total = total + feed_positions[1][:, None] * beam_directions[1][None, :]
    return total + feed_positions[2][:, None] * beam_directions[2][None, :]


def channel_flat(volt_chan, scale_chan, cosine, sine):
    scale_col = scale_chan.astype(jnp.float32)[:, None]
    weight_pair = jnp.concatenate([scale_col * cosine, scale_col * sine], axis=1).astype(
        jnp.bfloat16
    )
    row_block = volt_chan.astype(jnp.bfloat16).reshape(-1, volt_chan.shape[-1])
    product = jnp.dot(row_block, weight_pair, preferred_element_type=jnp.float32)
    beam_count = cosine.shape[1]
    product = product.reshape(2, 2, volt_chan.shape[2], 2, beam_count)
    real_part = product[0, :, :, 0] - product[1, :, :, 1]
    imag_part = product[0, :, :, 1] + product[1, :, :, 0]
    detected = (
        real_part[0] * real_part[0]
        + imag_part[0] * imag_part[0]
        + (real_part[1] * real_part[1] + imag_part[1] * imag_part[1])
    )
    detected = detected * POWER_SCALE
    return (detected - jnp.mean(detected, axis=0, keepdims=True)).astype(jnp.bfloat16)


def delay_table(dm_trials, chan_total, trial_count):
    chan_ids = jnp.arange(chan_total, dtype=jnp.int32)
    upper = jnp.int32(chan_total) + chan_ids
    sweeps = jnp.int32(256 * chan_total * chan_total) // (upper * upper) - jnp.int32(64)
    return (
        dm_trials[:, None] * sweeps[None, :] * jnp.int32(MAXD + 1) // jnp.int32(trial_count * 192)
    )


def dedisperse(extended, onehots, time_steps, scaling):
    chan_total = extended.shape[0]
    beam_items = extended.shape[2]
    accumulate = jnp.zeros((onehots[0].shape[0], time_steps * beam_items), jnp.float32)
    for shift_step in range(MAXD + 1):
        segment = extended[:, shift_step : shift_step + time_steps, :].reshape(
            chan_total, time_steps * beam_items
        )
        accumulate = accumulate + jnp.dot(
            onehots[shift_step], segment, preferred_element_type=jnp.float32
        )
    return (accumulate * scaling).reshape(onehots[0].shape[0], time_steps, beam_items)


def local(voltages, scales, feed_positions, beam_directions, dm_trials):
    chan_local = voltages.shape[0]
    window = voltages.shape[3]
    groups = lax.axis_size("chan")
    half_groups = groups // 2
    chan_total = groups * chan_local
    beam_count = beam_directions.shape[1]
    block_beams = beam_count // half_groups
    time_steps = window // 2
    trial_count = dm_trials.shape[0]
    scaling = 1.0 / math.sqrt(chan_total)
    geometry = geometry_delay(feed_positions, beam_directions)
    first_chan = lax.axis_index("chan") * chan_local
    frequency = first_chan.astype(jnp.float32) / chan_total + 1.0
    phase = TWO_PI * frequency * geometry
    cosine = jnp.cos(phase)
    sine = jnp.sin(phase)
    flat = lax.map(lambda items: channel_flat(items[0], items[1], cosine, sine), (voltages, scales))
    delays = delay_table(dm_trials, chan_total, trial_count)
    onehots = [(delays == shift_step).astype(jnp.bfloat16) for shift_step in range(MAXD + 1)]
    outgoing = flat.reshape(chan_local, 2, time_steps, half_groups, block_beams)
    outgoing = outgoing.transpose(1, 3, 0, 2, 4).reshape(
        groups, chan_local, time_steps, block_beams
    )
    arrived = lax.all_to_all(outgoing, "chan", split_axis=0, concat_axis=0, tiled=True)
    arrived_block = arrived.reshape(chan_total, time_steps, arrived.shape[3])
    tail_rows = passed_along(arrived_block[:, :MAXD, :], "chan", -half_groups)
    extended = jnp.concatenate([arrived_block, tail_rows], axis=1)
    result = dedisperse(extended, onehots, time_steps, scaling)
    return result.reshape(trial_count, 1, time_steps * block_beams)


def solution(mesh):
    return jax.shard_map(
        local,
        mesh=mesh,
        in_specs=(
            P(("grp", "chan"), None, None, None, None),
            P(("grp", "chan"), None),
            P(),
            P(),
            P(),
        ),
        out_specs=P(None, ("grp", "chan"), None),
        check_vma=False,
    )
```

profile of v0, /device:TPU:0, one launch (start us, length us, event | category | flops | bytes accessed | tf_op | source)
XLA Modules:
  0.0 111.3 jit_solution(13977786807538412760)
XLA Ops:
  1.7 71.5 %while.12 = (s32[]{:T(128)}, bf16[16,32,128]{2,1,0:T(8,128)(2,1)S(1)}, s32[16,2,2,32,1024]{4,3,2,1,0:T(8,128)}, s32[16,1024]{1,0:T(8,128)}, f32[128]{0:T(128)S(1...) while((s32[]{:T(128)}, ...), condition=%wide.region_2.3_spmd.clone.clone, body=%wide.region_0.2_spmd.clone.clone.sunk | while | flops 69661696 | bytes 3083917 | solution.py:87
  2.4 2.2 %fusion.189 = (bf16[1024,128]{0,1:T(8,128)(2,1)S(1)}, bf16[1024,128]{0,1:T(8,128)(2,1)S(1)}) fusion(f32[128]{0:T(128)S(1)} %get-tuple-element.290, f32[1024]{0:T(1024)S(1)} %get-tuple-element.291, f32[128]{0:T(128)S(1)} %get-tuple-element.288, f32[1024]{0:T(1024)S(1)} %get-tuple-element.289, f32[128]{0:T(128)S(1)} %get-tuple-element.286, ...), kind=kLoop, calls=%fused_computation.6.clone.1 | loop fusion | flops 1310720 | bytes 542212 | tf_op jit(solution)/shard_map/convert
  4.7 1.4 %fusion.190 = f32[2,2,32,2,128]{4,2,3,1,0:T(8,128)S(1)} fusion(bf16[2,128,1024,1,1]{2,1,0,4,3:T(8,128)(2,1)S(1)} %bitcast.78, s32[16,2,2,32,1024]{4,3,2,1,0:T(8,128)} %get-tuple-element.284, s32[]{:T(128)S(6)} %copy.19), kind=kOutput, calls=%fused_computation.10.clone.1 | convolution fusion | flops 67239936 | bytes 1179652 | tf_op jit(solution)/shard_map/while/body/eval_jaxpr/dot_general | solution.py:33
  6.9 2.2 %fusion.189 = (bf16[1024,128]{0,1:T(8,128)(2,1)S(1)}, bf16[1024,128]{0,1:T(8,128)(2,1)S(1)}) fusion(f32[128]{0:T(128)S(1)} %get-tuple-element.290, f32[1024]{0:T(1024)S(1)} %get-tuple-element.291, f32[128]{0:T(128)S(1)} %get-tuple-element.288, f32[1024]{0:T(1024)S(1)} %get-tuple-element.289, f32[128]{0:T(128)S(1)} %get-tuple-element.286, ...), kind=kLoop, calls=%fused_computation.6.clone.1 | loop fusion | flops 1310720 | bytes 542212 | tf_op jit(solution)/shard_map/convert
  9.2 1.4 %fusion.190 = f32[2,2,32,2,128]{4,2,3,1,0:T(8,128)S(1)} fusion(bf16[2,128,1024,1,1]{2,1,0,4,3:T(8,128)(2,1)S(1)} %bitcast.78, s32[16,2,2,32,1024]{4,3,2,1,0:T(8,128)} %get-tuple-element.284, s32[]{:T(128)S(6)} %copy.19), kind=kOutput, calls=%fused_computation.10.clone.1 | convolution fusion | flops 67239936 | bytes 1179652 | tf_op jit(solution)/shard_map/while/body/eval_jaxpr/dot_general | solution.py:33
  11.4 2.2 %fusion.189 = (bf16[1024,128]{0,1:T(8,128)(2,1)S(1)}, bf16[1024,128]{0,1:T(8,128)(2,1)S(1)}) fusion(f32[128]{0:T(128)S(1)} %get-tuple-element.290, f32[1024]{0:T(1024)S(1)} %get-tuple-element.291, f32[128]{0:T(128)S(1)} %get-tuple-element.288, f32[1024]{0:T(1024)S(1)} %get-tuple-element.289, f32[128]{0:T(128)S(1)} %get-tuple-element.286, ...), kind=kLoop, calls=%fused_computation.6.clone.1 | loop fusion | flops 1310720 | bytes 542212 | tf_op jit(solution)/shard_map/convert
  15.9 2.2 %fusion.189 = (bf16[1024,128]{0,1:T(8,128)(2,1)S(1)}, bf16[1024,128]{0,1:T(8,128)(2,1)S(1)}) fusion(f32[128]{0:T(128)S(1)} %get-tuple-element.290, f32[1024]{0:T(1024)S(1)} %get-tuple-element.291, f32[128]{0:T(128)S(1)} %get-tuple-element.288, f32[1024]{0:T(1024)S(1)} %get-tuple-element.289, f32[128]{0:T(128)S(1)} %get-tuple-element.286, ...), kind=kLoop, calls=%fused_computation.6.clone.1 | loop fusion | flops 1310720 | bytes 542212 | tf_op jit(solution)/shard_map/convert
  20.3 2.2 %fusion.189 = (bf16[1024,128]{0,1:T(8,128)(2,1)S(1)}, bf16[1024,128]{0,1:T(8,128)(2,1)S(1)}) fusion(f32[128]{0:T(128)S(1)} %get-tuple-element.290, f32[1024]{0:T(1024)S(1)} %get-tuple-element.291, f32[128]{0:T(128)S(1)} %get-tuple-element.288, f32[1024]{0:T(1024)S(1)} %get-tuple-element.289, f32[128]{0:T(128)S(1)} %get-tuple-element.286, ...), kind=kLoop, calls=%fused_computation.6.clone.1 | loop fusion | flops 1310720 | bytes 542212 | tf_op jit(solution)/shard_map/convert
  24.8 2.2 %fusion.189 = (bf16[1024,128]{0,1:T(8,128)(2,1)S(1)}, bf16[1024,128]{0,1:T(8,128)(2,1)S(1)}) fusion(f32[128]{0:T(128)S(1)} %get-tuple-element.290, f32[1024]{0:T(1024)S(1)} %get-tuple-element.291, f32[128]{0:T(128)S(1)} %get-tuple-element.288, f32[1024]{0:T(1024)S(1)} %get-tuple-element.289, f32[128]{0:T(128)S(1)} %get-tuple-element.286, ...), kind=kLoop, calls=%fused_computation.6.clone.1 | loop fusion | flops 1310720 | bytes 542212 | tf_op jit(solution)/shard_map/convert
  29.3 2.2 %fusion.189 = (bf16[1024,128]{0,1:T(8,128)(2,1)S(1)}, bf16[1024,128]{0,1:T(8,128)(2,1)S(1)}) fusion(f32[128]{0:T(128)S(1)} %get-tuple-element.290, f32[1024]{0:T(1024)S(1)} %get-tuple-element.291, f32[128]{0:T(128)S(1)} %get-tuple-element.288, f32[1024]{0:T(1024)S(1)} %get-tuple-element.289, f32[128]{0:T(128)S(1)} %get-tuple-element.286, ...), kind=kLoop, calls=%fused_computation.6.clone.1 | loop fusion | flops 1310720 | bytes 542212 | tf_op jit(solution)/shard_map/convert
  33.7 2.2 %fusion.189 = (bf16[1024,128]{0,1:T(8,128)(2,1)S(1)}, bf16[1024,128]{0,1:T(8,128)(2,1)S(1)}) fusion(f32[128]{0:T(128)S(1)} %get-tuple-element.290, f32[1024]{0:T(1024)S(1)} %get-tuple-element.291, f32[128]{0:T(128)S(1)} %get-tuple-element.288, f32[1024]{0:T(1024)S(1)} %get-tuple-element.289, f32[128]{0:T(128)S(1)} %get-tuple-element.286, ...), kind=kLoop, calls=%fused_computation.6.clone.1 | loop fusion | flops 1310720 | bytes 542212 | tf_op jit(solution)/shard_map/convert
  38.2 2.2 %fusion.189 = (bf16[1024,128]{0,1:T(8,128)(2,1)S(1)}, bf16[1024,128]{0,1:T(8,128)(2,1)S(1)}) fusion(f32[128]{0:T(128)S(1)} %get-tuple-element.290, f32[1024]{0:T(1024)S(1)} %get-tuple-element.291, f32[128]{0:T(128)S(1)} %get-tuple-element.288, f32[1024]{0:T(1024)S(1)} %get-tuple-element.289, f32[128]{0:T(128)S(1)} %get-tuple-element.286, ...), kind=kLoop, calls=%fused_computation.6.clone.1 | loop fusion | flops 1310720 | bytes 542212 | tf_op jit(solution)/shard_map/convert
  42.7 2.2 %fusion.189 = (bf16[1024,128]{0,1:T(8,128)(2,1)S(1)}, bf16[1024,128]{0,1:T(8,128)(2,1)S(1)}) fusion(f32[128]{0:T(128)S(1)} %get-tuple-element.290, f32[1024]{0:T(1024)S(1)} %get-tuple-element.291, f32[128]{0:T(128)S(1)} %get-tuple-element.288, f32[1024]{0:T(1024)S(1)} %get-tuple-element.289, f32[128]{0:T(128)S(1)} %get-tuple-element.286, ...), kind=kLoop, calls=%fused_computation.6.clone.1 | loop fusion | flops 1310720 | bytes 542212 | tf_op jit(solution)/shard_map/convert
  47.2 2.2 %fusion.189 = (bf16[1024,128]{0,1:T(8,128)(2,1)S(1)}, bf16[1024,128]{0,1:T(8,128)(2,1)S(1)}) fusion(f32[128]{0:T(128)S(1)} %get-tuple-element.290, f32[1024]{0:T(1024)S(1)} %get-tuple-element.291, f32[128]{0:T(128)S(1)} %get-tuple-element.288, f32[1024]{0:T(1024)S(1)} %get-tuple-element.289, f32[128]{0:T(128)S(1)} %get-tuple-element.286, ...), kind=kLoop, calls=%fused_computation.6.clone.1 | loop fusion | flops 1310720 | bytes 542212 | tf_op jit(solution)/shard_map/convert
  51.6 2.2 %fusion.189 = (bf16[1024,128]{0,1:T(8,128)(2,1)S(1)}, bf16[1024,128]{0,1:T(8,128)(2,1)S(1)}) fusion(f32[128]{0:T(128)S(1)} %get-tuple-element.290, f32[1024]{0:T(1024)S(1)} %get-tuple-element.291, f32[128]{0:T(128)S(1)} %get-tuple-element.288, f32[1024]{0:T(1024)S(1)} %get-tuple-element.289, f32[128]{0:T(128)S(1)} %get-tuple-element.286, ...), kind=kLoop, calls=%fused_computation.6.clone.1 | loop fusion | flops 1310720 | bytes 542212 | tf_op jit(solution)/shard_map/convert
  56.1 2.2 %fusion.189 = (bf16[1024,128]{0,1:T(8,128)(2,1)S(1)}, bf16[1024,128]{0,1:T(8,128)(2,1)S(1)}) fusion(f32[128]{0:T(128)S(1)} %get-tuple-element.290, f32[1024]{0:T(1024)S(1)} %get-tuple-element.291, f32[128]{0:T(128)S(1)} %get-tuple-element.288, f32[1024]{0:T(1024)S(1)} %get-tuple-element.289, f32[128]{0:T(128)S(1)} %get-tuple-element.286, ...), kind=kLoop, calls=%fused_computation.6.clone.1 | loop fusion | flops 1310720 | bytes 542212 | tf_op jit(solution)/shard_map/convert
  60.6 2.2 %fusion.189 = (bf16[1024,128]{0,1:T(8,128)(2,1)S(1)}, bf16[1024,128]{0,1:T(8,128)(2,1)S(1)}) fusion(f32[128]{0:T(128)S(1)} %get-tuple-element.290, f32[1024]{0:T(1024)S(1)} %get-tuple-element.291, f32[128]{0:T(128)S(1)} %get-tuple-element.288, f32[1024]{0:T(1024)S(1)} %get-tuple-element.289, f32[128]{0:T(128)S(1)} %get-tuple-element.286, ...), kind=kLoop, calls=%fused_computation.6.clone.1 | loop fusion | flops 1310720 | bytes 542212 | tf_op jit(solution)/shard_map/convert
  65.0 2.2 %fusion.189 = (bf16[1024,128]{0,1:T(8,128)(2,1)S(1)}, bf16[1024,128]{0,1:T(8,128)(2,1)S(1)}) fusion(f32[128]{0:T(128)S(1)} %get-tuple-element.290, f32[1024]{0:T(1024)S(1)} %get-tuple-element.291, f32[128]{0:T(128)S(1)} %get-tuple-element.288, f32[1024]{0:T(1024)S(1)} %get-tuple-element.289, f32[128]{0:T(128)S(1)} %get-tuple-element.286, ...), kind=kLoop, calls=%fused_computation.6.clone.1 | loop fusion | flops 1310720 | bytes 542212 | tf_op jit(solution)/shard_map/convert
  69.5 2.2 %fusion.189 = (bf16[1024,128]{0,1:T(8,128)(2,1)S(1)}, bf16[1024,128]{0,1:T(8,128)(2,1)S(1)}) fusion(f32[128]{0:T(128)S(1)} %get-tuple-element.290, f32[1024]{0:T(1024)S(1)} %get-tuple-element.291, f32[128]{0:T(128)S(1)} %get-tuple-element.288, f32[1024]{0:T(1024)S(1)} %get-tuple-element.289, f32[128]{0:T(128)S(1)} %get-tuple-element.286, ...), kind=kLoop, calls=%fused_computation.6.clone.1 | loop fusion | flops 1310720 | bytes 542212 | tf_op jit(solution)/shard_map/convert
  71.8 1.4 %fusion.190 = f32[2,2,32,2,128]{4,2,3,1,0:T(8,128)S(1)} fusion(bf16[2,128,1024,1,1]{2,1,0,4,3:T(8,128)(2,1)S(1)} %bitcast.78, s32[16,2,2,32,1024]{4,3,2,1,0:T(8,128)} %get-tuple-element.284, s32[]{:T(128)S(6)} %copy.19), kind=kOutput, calls=%fused_computation.10.clone.1 | convolution fusion | flops 67239936 | bytes 1179652 | tf_op jit(solution)/shard_map/while/body/eval_jaxpr/dot_general | solution.py:33
  74.1 1.8 %reshape.148 = bf16[16,2,2048]{2,1,0:T(2,128)(2,1)} reshape(bf16[16,16,16,16]{3,2,1,0:T(8,128)(2,1)S(1)} %bitcast.81) | data formatting | bytes 262144
  75.8 7.4 %all-to-all-start = ((bf16[16,2,2048]{2,1,0:T(2,128)(2,1)}), bf16[16,2,2048]{2,1,0:T(2,128)(2,1)S(1)}, u32[]{:S(2)}, u32[]{:S(2)}) async-start(bf16[16,2,2048]{2,1,0:T(2,128)(2,1)} %reshape.148), calls=%async_computation | async-start | bytes 262144 | tf_op jit(solution)/shard_map/all_to_all | solution.py:94
  83.3 7.8 %all-to-all-done = bf16[16,2,2048]{2,1,0:T(2,128)(2,1)S(1)} async-done(((bf16[16,2,2048]{2,1,0:T(2,128)(2,1)}), bf16[16,2,2048]{2,1,0:T(2,128)(2,1)S(1)}, u32[]{:S(2)}, u32[]{:S(2)}) %all-to-all-start) | async-done | bytes 131104 | tf_op jit(solution)/shard_map/all_to_all | solution.py:94
  95.4 8.3 %collective-permute-done = bf16[256,15,16]{0,2,1:T(8,128)(2,1)S(1)} collective-permute-done((bf16[256,15,16]{0,2,1:T(8,128)(2,1)S(1)}, bf16[256,15,16]{0,2,1:T(8,128)(2,1)S(1)}, u32[]{:S(2)}, u32[]{:S(2)}) %collective-permute-start) | collective-permute-done | bytes 122912 | tf_op jit(solution)/shard_map/ppermute | solution.py:18
  (141 shorter events, 46.0 us)
Async XLA Ops:
  1.6 93.3 %copy-start = (s32[256]{0:T(256)S(1)}, s32[256]{0:T(256)}, u32[]{:S(2)}) copy-start(s32[256]{0:T(256)} %param.11) | copy-start | bytes 3076
  75.8 15.3 %all-to-all-start = ((bf16[16,2,2048]{2,1,0:T(2,128)(2,1)}), bf16[16,2,2048]{2,1,0:T(2,128)(2,1)S(1)}, u32[]{:S(2)}, u32[]{:S(2)}) async-start(bf16[16,2,2048]{2,1,0:T(2,128)(2,1)} %reshape.148), calls=%async_computation | async-start | bytes 262144 | tf_op jit(solution)/shard_map/all_to_all | solution.py:94
  93.7 10.0 %collective-permute-start = (bf16[256,15,16]{0,2,1:T(8,128)(2,1)S(1)}, bf16[256,15,16]{0,2,1:T(8,128)(2,1)S(1)}, u32[]{:S(2)}, u32[]{:S(2)}) collective-permute-start(bf16[256,15,16]{0,2,1:T(8,128)(2,1)S(1)} %slice.144), channel_id=1, source_target_pairs={{8,0},{9,1},{10,2},{11,3},{12,4},{13,5},{14,6},{15,7},{24,16},{25,... | collective-permute-start | bytes 368648 | tf_op jit(solution)/shard_map/ppermute | solution.py:18
where the time goes:
time: 113 us; the launch traced here: 111 us
  other arithmetic  49.3 us (44%)
  matrix products  28.6 us (25%)
  waiting for transfers between devices  16.1 us (14%)
  starting transfers between devices  8.67 us (8%)
  local copies, waits for them, and re-layouts  7.75 us (7%)
    another operation x16, other arithmetic  35.1 us
    dot_general x16, matrix products, channel_flat(): jnp.dot(row_block, weight_pair, preferred_element_type=jnp.float32)  21.7 us
    convert_element_type x16, other arithmetic, channel_flat(): scale_col = scale_chan.astype(jnp.float32)[:, None]  12.3 us
    ppermute x1, waiting for transfers between devices, passed_along(): lax.ppermute(value, axis, [(source, source + steps) for source in range(l...  8.26 us
    all_to_all x1, waiting for transfers between devices, local(): lax.all_to_all(outgoing, 'chan', split_axis=0, concat_axis=0, tiled=True)  7.81 us
    all_to_all x1, starting transfers between devices, local(): lax.all_to_all(outgoing, 'chan', split_axis=0, concat_axis=0, tiled=True)  7.38 us
    dot_general x16, matrix products, dedisperse(): jnp.dot(onehots[shift_step], segment, preferred_element_type=jnp.float32)  6.9 us
    unnamed x4, local copies, waits for them, and re-layouts  2.46 us
  transfers between devices with their start and end apart: 2, of which 2 were waited for; matrix products, arithmetic and copies ran while one was open for 0% of the time, Pallas kernels for 0%

commit v1 on v0

v1 whole, which is shorter than its diff:
```python
import functools
import math

import numpy as np

import jax
import jax.numpy as jnp
from jax import lax
from jax.experimental import pallas as pl
from jax.experimental.pallas import tpu as pltpu
from jax.sharding import PartitionSpec as P

MAXD = 15
POWER_SCALE = 1.0 / 67108864.0
LANES = 128
CHANS = 16
OCTET = 8
VMEM_LIMIT = 48 * 1024 * 1024

SIN_TERMS = [(-1) ** k * (2 * math.pi) ** (2 * k + 1) / math.factorial(2 * k + 1) for k in range(5)]
COS_TERMS = [(-1) ** k * (2 * math.pi) ** (2 * k) / math.factorial(2 * k) for k in range(6)]


def horner(terms, square):
    total = jnp.full_like(square, terms[-1])
    for term in terms[-2::-1]:
        total = total * square + jnp.float32(term)
    return total


def cos_sin_turns(turns):
    quarters = jnp.round(turns * 4.0)
    rest = turns - quarters * 0.25
    square = rest * rest
    sine = horner(SIN_TERMS, square) * rest
    cosine = horner(COS_TERMS, square)
    which = quarters.astype(jnp.int32)
    swap = (which & 1) == 1
    base_cos = jnp.where(swap, sine, cosine)
    base_sin = jnp.where(swap, cosine, sine)
    cos_out = jnp.where(((which + 1) & 2) == 2, -base_cos, base_cos)
    sin_out = jnp.where((which & 2) == 2, -base_sin, base_sin)
    return cos_out, sin_out


def swap_lanes_and_list(tiles, width):
    count = len(tiles)
    lane = lax.broadcasted_iota(jnp.int32, tiles[0].shape, 1)
    tiles = list(tiles)
    step = count // 2
    while step >= 1:
        upper = ((lane // (step * width)) & 1) == 1
        for low in range(count):
            if low & step:
                continue
            a, b = tiles[low], tiles[low + step]
            tiles[low] = jnp.where(upper, pltpu.roll(b, step * width, 1), a)
            tiles[low + step] = jnp.where(upper, b, pltpu.roll(a, LANES - step * width, 1))
        step //= 2
    return tiles


def beam_kernel(chan_total, volt_hbm, scales_ref, pos_ref, dirs_ref, out_ref, volt, cosine, sine, power, sems):
    block = pl.program_id(0)
    copies = [pltpu.make_async_copy(volt_hbm.at[c], volt.at[c], sems.at[c]) for c in range(CHANS)]

    @pl.when(block == 0)
    def _():
        for copy in copies:
            copy.start()

    first_chan = lax.axis_index("chan") * CHANS
    frequency = first_chan.astype(jnp.float32) / chan_total + 1.0
    columns = jnp.transpose(jnp.concatenate([dirs_ref[...], jnp.zeros((5, LANES), jnp.float32)], axis=0))
    feeds = pos_ref.shape[1]
    for start in range(0, feeds, LANES):
        at = slice(start, start + LANES)
        geometry = pos_ref[0:1, at] * columns[:, 0:1]
        geometry = geometry + pos_ref[1:2, at] * columns[:, 1:2]
        geometry = geometry + pos_ref[2:3, at] * columns[:, 2:3]
        cosine[:, at], sine[:, at] = cos_sin_turns(frequency * geometry)

    window = volt.shape[3]
    for c in range(CHANS):
        @pl.when(block == 0)
        def _():
            copies[c].wait()

        rows = volt[c].reshape(4 * window, feeds).astype(jnp.float32).astype(jnp.bfloat16)
        scale = scales_ref[c : c + 1, :].astype(jnp.float32)
        weights = jnp.concatenate([(scale * cosine[...]).astype(jnp.bfloat16), (scale * sine[...]).astype(jnp.bfloat16)], axis=0)
        product = lax.dot_general(rows, weights, (((1,), (1,)), ((), ())), preferred_element_type=jnp.float32)
        half = 2 * window
        real = product[:half, :LANES] - product[half:, LANES:]
        imag = product[:half, LANES:] + product[half:, :LANES]
        both = real * real + imag * imag
        detected = both[:window] + both[window:]
        flat = detected - jnp.mean(detected, axis=0, keepdims=True)
        power[pl.ds(c, window, stride=CHANS), :] = flat

    zeros = jnp.zeros((2 * CHANS, LANES), jnp.bfloat16)
    for octet in range(window // OCTET):
        tiles = [power[(octet * OCTET + t) * CHANS : (octet * OCTET + t + 1) * CHANS, :] for t in range(OCTET)]
        tiles = swap_lanes_and_list(tiles, CHANS)
        for h in range(OCTET):
            tile = tiles[h].astype(jnp.bfloat16)
            out_ref[0, h, octet * CHANS : (octet + 1) * CHANS, :] = tile
            if octet >= 2:
                out_ref[1, h, (octet - 2) * CHANS : (octet - 1) * CHANS, :] = tile
    for h in range(OCTET):
        out_ref[1, h, 2 * CHANS :, :] = zeros


def beams(voltages, scales, feed_positions, beam_directions, chan_total):
    window, feeds = voltages.shape[3:]
    beam_count = beam_directions.shape[1]
    blocks = beam_count // LANES
    return pl.pallas_call(
        functools.partial(beam_kernel, chan_total),
        grid=(blocks,),
        in_specs=[
            pl.BlockSpec(memory_space=pl.ANY),
            pl.BlockSpec((CHANS, feeds), lambda i: (0, 0)),
            pl.BlockSpec((3, feeds), lambda i: (0, 0)),
            pl.BlockSpec((3, LANES), lambda i: (0, i)),
        ],
        out_specs=pl.BlockSpec((2, OCTET, 4 * CHANS, LANES), lambda i: (0, i, 0, 0)),
        out_shape=jax.ShapeDtypeStruct((2, blocks * OCTET, 4 * CHANS, LANES), jnp.bfloat16),
        scratch_shapes=[
            pltpu.VMEM(voltages.shape, jnp.int32),
            pltpu.VMEM((LANES, feeds), jnp.float32),
            pltpu.VMEM((LANES, feeds), jnp.float32),
            pltpu.VMEM((window * CHANS, LANES), jnp.float32),
            pltpu.SemaphoreType.DMA((CHANS,)),
        ],
        compiler_params=pltpu.CompilerParams(vmem_limit_bytes=VMEM_LIMIT),
        name="beams",
    )(voltages, scales, feed_positions, beam_directions)


def dedisperse_kernel(scaling, divisor, arrived_ref, sweeps_ref, dm_ref, out_ref, masks, pieces):
    trials = out_ref.shape[0]
    part = pl.program_id(0)
    delays = (dm_ref[...] * sweeps_ref[...]) // divisor
    depth = delays.shape[1]
    tiles = [arrived_ref[:, o * CHANS : (o + 1) * CHANS, :].reshape(depth, LANES).astype(jnp.float32) for o in range(4)]
    lane = lax.broadcasted_iota(jnp.int32, (depth, LANES), 1)
    for r in range(OCTET):
        if r == 0:
            moved = tiles[:3]
        else:
            rolled = [pltpu.roll(tile, LANES - r * CHANS, 1) for tile in tiles]
            moved = [jnp.where(lane < LANES - r * CHANS, rolled[o], rolled[o + 1]) for o in range(3)]
        moved = [tile.astype(jnp.bfloat16) for tile in moved]
        for a in range(2):
            shift = OCTET * a + r
            masks[:, shift * depth : (shift + 1) * depth] = jnp.where(delays == shift, 1.0, 0.0).astype(jnp.bfloat16)
            pieces[shift * depth : (shift + 1) * depth, :LANES] = moved[a]
            pieces[shift * depth : (shift + 1) * depth, LANES:] = moved[a + 1]
    total = jnp.dot(masks[...], pieces[...], preferred_element_type=jnp.float32) * scaling

    @pl.when(part == 0)
    def _():
        out_ref[...] = total

    @pl.when(part > 0)
    def _():
        out_ref[...] += total


def dedisperse(arrived, dm_trials, chan_total):
    sources = arrived.shape[0]
    trials = dm_trials.shape[0]
    ids = np.arange(chan_total, dtype=np.int64)
    sweeps = ((256 * chan_total * chan_total) // ((chan_total + ids) ** 2) - 64).astype(np.int32)
    group = min(sources, 16)
    depth = group * CHANS
    scaling = POWER_SCALE / math.sqrt(chan_total)
    divisor = trials * 192 // (MAXD + 1)
    return pl.pallas_call(
        functools.partial(dedisperse_kernel, scaling, divisor),
        grid=(sources // group,),
        in_specs=[
            pl.BlockSpec((group, 4 * CHANS, LANES), lambda i: (i, 0, 0)),
            pl.BlockSpec((1, depth), lambda i: (0, i)),
            pl.BlockSpec((trials, 1), lambda i: (0, 0)),
        ],
        out_specs=pl.BlockSpec((trials, 2 * LANES), lambda i: (0, 0)),
        out_shape=jax.ShapeDtypeStruct((trials, 2 * LANES), jnp.float32),
        scratch_shapes=[
            pltpu.VMEM((trials, (MAXD + 1) * depth), jnp.bfloat16),
            pltpu.VMEM(((MAXD + 1) * depth, 2 * LANES), jnp.bfloat16),
        ],
        compiler_params=pltpu.CompilerParams(vmem_limit_bytes=VMEM_LIMIT),
        name="dedisperse",
    )(arrived, jnp.asarray(sweeps)[None, :], dm_trials[:, None])


def local(voltages, scales, feed_positions, beam_directions, dm_trials):
    groups = lax.axis_size("chan")
    chan_total = groups * voltages.shape[0]
    outgoing = beams(voltages, scales, feed_positions, beam_directions, chan_total)
    outgoing = outgoing.reshape(groups, 4 * CHANS, LANES)
    arrived = lax.all_to_all(outgoing, "chan", split_axis=0, concat_axis=0, tiled=True)
    result = dedisperse(arrived, dm_trials, chan_total)
    return result[:, None, :]


def solution(mesh):
    return jax.shard_map(
        local,
        mesh=mesh,
        in_specs=(
            P(("grp", "chan"), None, None, None, None),
            P(("grp", "chan"), None),
            P(),
            P(),
            P(),
        ),
        out_specs=P(None, ("grp", "chan"), None),
        check_vma=False,
    )
```

time: 113 us -> 31.6 us (0.28); the launches traced: 111 us -> 31.3 us
  other arithmetic: 49.3 us -> 0 us
  matrix products: 28.6 us -> 0 us
  Pallas kernels: 0 us -> 10.6 us
  waiting for transfers between devices: 16.1 us -> 9.9 us
  local copies, waits for them, and re-layouts: 7.75 us -> 3.35 us
  starting transfers between devices: 8.67 us -> 7.4 us
    another operation x16 -> x0, other arithmetic: 35.1 us -> none
    dot_general x32 -> x0, matrix products: 28.6 us -> none  [the longest x16 21.7 us: channel_flat(): jnp.dot(row_block, weight_pair, preferred_element_type=jnp.float32)]
    convert_element_type x16 -> x0, other arithmetic: 12.3 us -> none  [channel_flat(): scale_col = scale_chan.astype(jnp.float32)[:, None]]
    pallas_call x0 -> x2, Pallas kernels: none -> 10.6 us  [the longest x1 9.44 us: beams(): pl.pallas_call(functools.partial(beam_kernel, chan_total), grid=(blocks,)...]
    ppermute x1 -> x0, waiting for transfers between devices: 8.26 us -> none  [passed_along(): lax.ppermute(value, axis, [(source, source + steps) for source in range(l...]
    all_to_all x1, waiting for transfers between devices: 7.81 us -> 9.9 us  [local(): lax.all_to_all(outgoing, 'chan', split_axis=0, concat_axis=0, tiled=True)]
    another operation x2 -> x0, local copies, waits for them, and re-layouts: 1.97 us -> none  [the longest x1 0.99 us: dedisperse(): extended[:, shift_step:shift_step + time_steps, :]]
    reshape x2 -> x0, local copies, waits for them, and re-layouts: 1.49 us -> none  [the longest x1 0.83 us: local(): arrived_block = arrived.reshape(chan_total, time_steps, arrived.shape[3])]
  transfers between devices with their start and end apart: 2 -> 1, of which waited for: 2 -> 1; matrix products, arithmetic and copies ran while one was open for 0% -> 0% of each run, Pallas kernels for 0% -> 0%
where the time goes in v1:
time: 31.6 us; the launch traced here: 31.3 us
  Pallas kernels  10.6 us (34%)
  waiting for transfers between devices  9.9 us (31%)
  starting transfers between devices  7.4 us (23%)
  local copies, waits for them, and re-layouts  3.35 us (11%)
    all_to_all x1, waiting for transfers between devices, local(): lax.all_to_all(outgoing, 'chan', split_axis=0, concat_axis=0, tiled=True)  9.9 us
    pallas_call x1, Pallas kernels, beams(): pl.pallas_call(functools.partial(beam_kernel, chan_total), grid=(blocks,)...  9.44 us
    all_to_all x1, starting transfers between devices, local(): lax.all_to_all(outgoing, 'chan', split_axis=0, concat_axis=0, tiled=True)  7.4 us
    unnamed x10, local copies, waits for them, and re-layouts  2.24 us
    pallas_call x1, Pallas kernels, dedisperse(): pl.pallas_call(functools.partial(dedisperse_kernel, scaling, divisor), gr...  1.13 us
    broadcast_in_dim x1, local copies, waits for them, and re-layouts, local(): return result[:, None, :]  0.97 us
  transfers between devices with their start and end apart: 1, of which 1 were waited for; matrix products, arithmetic and copies ran while one was open for 0% of the time, Pallas kernels for 0%

profile of v1, /device:TPU:0, one launch (start us, length us, event | category | flops | bytes accessed | tf_op | source)
XLA Modules:
  0.0 31.3 jit_solution(8641558828150972724)
XLA Ops:
  0.0 0.0 copy-start
  0.0 0.8 %copy-done = s32[16,1024]{1,0:T(8,128)S(1)} copy-done((s32[16,1024]{1,0:T(8,128)S(1)}, s32[16,1024]{1,0:T(8,128)}, u32[]{:S(2)}) %copy-start) | copy-done | bytes 65560
  0.8 0.0 copy-start.1
  0.8 0.7 %copy-done.1 = f32[3,1024]{1,0:T(4,128)S(1)} copy-done((f32[3,1024]{1,0:T(4,128)S(1)}, f32[3,1024]{1,0:T(4,128)}, u32[]{:S(2)}) %copy-start.1) | copy-done | bytes 12312
  1.6 0.0 copy-start.2
  1.6 0.7 %copy-done.2 = f32[3,128]{1,0:T(4,128)S(1)} copy-done((f32[3,128]{1,0:T(4,128)S(1)}, f32[3,128]{1,0:T(4,128)}, u32[]{:S(2)}) %copy-start.2) | copy-done | bytes 1560
  2.2 0.0 copy-start.4
  2.2 0.0 copy-start.3
  2.2 9.4 %beams.1 = bf16[2,8,64,128]{3,2,1,0:T(8,128)(2,1)} custom-call(s32[16,2,2,32,1024]{4,3,2,1,0:T(8,128)} %volt_hbm.1, s32[16,1024]{1,0:T(8,128)S(1)} %copy-done, f32[3,1024]{1,0:T(4,128)S(1)} %copy-done.1, f32[3,128]{1,0:T(4,128)S(1)} %copy-done.2), custom_call_target="tpu_custom_call" | custom-call | tf_op jit(solution)/shard_map/beams/pallas_call | solution.py:118
  11.7 7.4 %all-to-all-start = ((bf16[16,64,128]{2,1,0:T(8,128)(2,1)}), bf16[16,64,128]{2,1,0:T(8,128)(2,1)S(1)}, u32[]{:S(2)}, u32[]{:S(2)}) async-start(bf16[16,64,128]{2,1,0:T(8,128)(2,1)} %bitcast), calls=%async_computation | async-start | bytes 524288 | tf_op jit(solution)/shard_map/all_to_all | solution.py:204
  19.1 0.0 copy-done.4
  19.1 0.1 copy.8.dm_ref
  19.2 9.9 %all-to-all-done.arrived_ref = bf16[16,64,128]{2,1,0:T(8,128)(2,1)S(1)} async-done(((bf16[16,64,128]{2,1,0:T(8,128)(2,1)}), bf16[16,64,128]{2,1,0:T(8,128)(2,1)S(1)}, u32[]{:S(2)}, u32[]{:S(2)}) %all-to-all-start) | async-done | bytes 262176 | tf_op jit(solution)/shard_map/all_to_all | solution.py:204
  29.1 0.0 copy-done.3
  29.1 1.1 %dedisperse.1 = f32[256,256]{1,0:T(8,128)S(1)} custom-call(bf16[16,64,128]{2,1,0:T(8,128)(2,1)S(1)} %all-to-all-done.arrived_ref, s32[1,256]{1,0:T(1,128)S(1)} %copy-done.3, s32[256,1]{1,0:T(8,128)S(1)} %copy.8.dm_ref), custom_call_target="tpu_custom_call" | custom-call | tf_op jit(solution)/shard_map/dedisperse/pallas_call | solution.py:180
  30.3 1.0 %copy.9 = f32[256,1,256]{2,1,0:T(1,128)} copy(f32[256,1,256]{2,0,1:T(8,128)S(1)} %bitcast.3) | data formatting | bytes 524288 | tf_op jit(solution)/shard_map/broadcast_in_dim | solution.py:206
Async XLA Ops:
  0.0 0.8 %copy-start = (s32[16,1024]{1,0:T(8,128)S(1)}, s32[16,1024]{1,0:T(8,128)}, u32[]{:S(2)}) copy-start(s32[16,1024]{1,0:T(8,128)} %scales_ref.1) | copy-start | bytes 196612
  0.8 0.7 %copy-start.1 = (f32[3,1024]{1,0:T(4,128)S(1)}, f32[3,1024]{1,0:T(4,128)}, u32[]{:S(2)}) copy-start(f32[3,1024]{1,0:T(4,128)} %pos_ref.1) | copy-start | bytes 36868
  1.6 0.7 %copy-start.2 = (f32[3,128]{1,0:T(4,128)S(1)}, f32[3,128]{1,0:T(4,128)}, u32[]{:S(2)}) copy-start(f32[3,128]{1,0:T(4,128)} %dirs_ref.1) | copy-start | bytes 4612
  2.2 16.9 %copy-start.4 = (s32[256]{0:T(256)S(1)}, s32[256]{0:T(256)}, u32[]{:S(2)}) copy-start(s32[256]{0:T(256)} %param.10) | copy-start | bytes 3076
  2.2 26.9 %copy-start.3 = (s32[1,256]{1,0:T(1,128)S(1)}, s32[1,256]{1,0:T(1,128)}, u32[]{:S(2)}) copy-start(s32[1,256]{1,0:T(1,128)} %constant.5.sweeps_ref) | copy-start | bytes 3076
  11.7 17.5 %all-to-all-start = ((bf16[16,64,128]{2,1,0:T(8,128)(2,1)}), bf16[16,64,128]{2,1,0:T(8,128)(2,1)S(1)}, u32[]{:S(2)}, u32[]{:S(2)}) async-start(bf16[16,64,128]{2,1,0:T(8,128)(2,1)} %bitcast), calls=%async_computation | async-start | bytes 524288 | tf_op jit(solution)/shard_map/all_to_all | solution.py:204

commit v2 on v1

--- a/solution.py
+++ b/solution.py
@@ -15,7 +15,10 @@
 LANES = 128
 CHANS = 16
 OCTET = 8
-VMEM_LIMIT = 48 * 1024 * 1024
+BATCHES = (4, 4, 4, 4)
+DEPTH = 256
+BEAM_VMEM = 40 * 1024 * 1024
+VMEM_LIMIT = 24 * 1024 * 1024
 
 SIN_TERMS = [(-1) ** k * (2 * math.pi) ** (2 * k + 1) / math.factorial(2 * k + 1) for k in range(5)]
 COS_TERMS = [(-1) ** k * (2 * math.pi) ** (2 * k) / math.factorial(2 * k) for k in range(6)]
@@ -60,36 +63,64 @@
     return tiles
 
 
-def beam_kernel(chan_total, volt_hbm, scales_ref, pos_ref, dirs_ref, out_ref, volt, cosine, sine, power, sems):
-    block = pl.program_id(0)
-    copies = [pltpu.make_async_copy(volt_hbm.at[c], volt.at[c], sems.at[c]) for c in range(CHANS)]
-
-    @pl.when(block == 0)
-    def _():
-        for copy in copies:
+def in_first_block(blocks, action):
+    if blocks == 1:
+        action()
+    else:
+        pl.when(pl.program_id(0) == 0)(action)
+
+
+def channel_product(volt, c, scale_columns, cosine, sine, window, feeds):
+    total = None
+    for low in range(0, feeds, DEPTH):
+        at = slice(low, low + DEPTH)
+        rows = volt[c, :, :, :, at].reshape(4 * window, DEPTH).astype(jnp.float32).astype(jnp.bfloat16)
+        scale = jnp.broadcast_to(scale_columns[at, c : c + 1], (DEPTH, LANES)).astype(jnp.float32)
+        weights = jnp.concatenate([(scale * cosine[at, :]).astype(jnp.bfloat16), (scale * sine[at, :]).astype(jnp.bfloat16)], axis=1)
+        part = jnp.dot(rows, weights, preferred_element_type=jnp.float32)
+        total = part if total is None else total + part
+    return total
+
+
+def beam_kernel(chan_total, blocks, volt_hbm, scales_hbm, pos_hbm, dirs_hbm, out_ref, volt, scales, pos, dirs, cosine, sine, power, sems, small_sems):
+    edges = [sum(BATCHES[:k]) for k in range(len(BATCHES) + 1)]
+    small = [
+        pltpu.make_async_copy(source, target, small_sems.at[k])
+        for k, (source, target) in enumerate(((pos_hbm, pos), (dirs_hbm, dirs), (scales_hbm, scales)))
+    ]
+    copies = [
+        pltpu.make_async_copy(volt_hbm.at[low:high], volt.at[low:high], sems.at[k])
+        for k, (low, high) in enumerate(zip(edges, edges[1:]))
+    ]
+
+    def start_all():
+        for copy in small + copies:
             copy.start()
+        for copy in small:
+            copy.wait()
+
+    in_first_block(blocks, start_all)
 
     first_chan = lax.axis_index("chan") * CHANS
     frequency = first_chan.astype(jnp.float32) / chan_total + 1.0
-    columns = jnp.transpose(jnp.concatenate([dirs_ref[...], jnp.zeros((5, LANES), jnp.float32)], axis=0))
-    feeds = pos_ref.shape[1]
-    for start in range(0, feeds, LANES):
-        at = slice(start, start + LANES)
-        geometry = pos_ref[0:1, at] * columns[:, 0:1]
-        geometry = geometry + pos_ref[1:2, at] * columns[:, 1:2]
-        geometry = geometry + pos_ref[2:3, at] * columns[:, 2:3]
-        cosine[:, at], sine[:, at] = cos_sin_turns(frequency * geometry)
+    feeds = pos.shape[1]
+    places = jnp.transpose(jnp.concatenate([pos[...], jnp.zeros((5, feeds), jnp.float32)], axis=0))
+    if blocks == 1:
+        beam_rows = dirs[...]
+    else:
+        beam_rows = dirs[:, pl.ds(pl.multiple_of(pl.program_id(0) * LANES, LANES), LANES)]
+    geometry = places[:, 0:1] * beam_rows[0:1, :]
+    geometry = geometry + places[:, 1:2] * beam_rows[1:2, :]
+    geometry = geometry + places[:, 2:3] * beam_rows[2:3, :]
+    cosine[...], sine[...] = cos_sin_turns(frequency * geometry)
+    scale_columns = jnp.transpose(scales[...].astype(jnp.float32)).astype(jnp.bfloat16)
 
     window = volt.shape[3]
     for c in range(CHANS):
-        @pl.when(block == 0)
-        def _():
-            copies[c].wait()
-
-        rows = volt[c].reshape(4 * window, feeds).astype(jnp.float32).astype(jnp.bfloat16)
-        scale = scales_ref[c : c + 1, :].astype(jnp.float32)
-        weights = jnp.concatenate([(scale * cosine[...]).astype(jnp.bfloat16), (scale * sine[...]).astype(jnp.bfloat16)], axis=0)
-        product = lax.dot_general(rows, weights, (((1,), (1,)), ((), ())), preferred_element_type=jnp.float32)
+        if c in edges:
+            in_first_block(blocks, copies[edges.index(c)].wait)
+
+        product = channel_product(volt, c, scale_columns, cosine, sine, window, feeds)
         half = 2 * window
         real = product[:half, :LANES] - product[half:, LANES:]
         imag = product[:half, LANES:] + product[half:, :LANES]
@@ -116,32 +147,37 @@
     beam_count = beam_directions.shape[1]
     blocks = beam_count // LANES
     return pl.pallas_call(
-        functools.partial(beam_kernel, chan_total),
+        functools.partial(beam_kernel, chan_total, blocks),
         grid=(blocks,),
         in_specs=[
             pl.BlockSpec(memory_space=pl.ANY),
-            pl.BlockSpec((CHANS, feeds), lambda i: (0, 0)),
-            pl.BlockSpec((3, feeds), lambda i: (0, 0)),
-            pl.BlockSpec((3, LANES), lambda i: (0, i)),
+            pl.BlockSpec(memory_space=pl.ANY),
+            pl.BlockSpec(memory_space=pl.ANY),
+            pl.BlockSpec(memory_space=pl.ANY),
         ],
         out_specs=pl.BlockSpec((2, OCTET, 4 * CHANS, LANES), lambda i: (0, i, 0, 0)),
         out_shape=jax.ShapeDtypeStruct((2, blocks * OCTET, 4 * CHANS, LANES), jnp.bfloat16),
         scratch_shapes=[
             pltpu.VMEM(voltages.shape, jnp.int32),
-            pltpu.VMEM((LANES, feeds), jnp.float32),
-            pltpu.VMEM((LANES, feeds), jnp.float32),
+            pltpu.VMEM(scales.shape, jnp.int32),
+            pltpu.VMEM(feed_positions.shape, jnp.float32),
+            pltpu.VMEM(beam_directions.shape, jnp.float32),
+            pltpu.VMEM((feeds, LANES), jnp.float32),
+            pltpu.VMEM((feeds, LANES), jnp.float32),
             pltpu.VMEM((window * CHANS, LANES), jnp.float32),
-            pltpu.SemaphoreType.DMA((CHANS,)),
-        ],
-        compiler_params=pltpu.CompilerParams(vmem_limit_bytes=VMEM_LIMIT),
+            pltpu.SemaphoreType.DMA((len(BATCHES),)),
+            pltpu.SemaphoreType.DMA((3,)),
+        ],
+        compiler_params=pltpu.CompilerParams(vmem_limit_bytes=BEAM_VMEM),
         name="beams",
-    )(voltages, scales, feed_positions, beam_directions)
+    )(*(pltpu.with_memory_space_constraint(x, pltpu.HBM) for x in (voltages, scales, feed_positions, beam_directions)))
 
 
 def dedisperse_kernel(scaling, divisor, arrived_ref, sweeps_ref, dm_ref, out_ref, masks, pieces):
     trials = out_ref.shape[0]
     part = pl.program_id(0)
-    delays = (dm_ref[...] * sweeps_ref[...]) // divisor
+    product = (dm_ref[...] * sweeps_ref[...]).astype(jnp.float32)
+    delays = jnp.floor((product + 0.5) * (1.0 / divisor))
     depth = delays.shape[1]
     tiles = [arrived_ref[:, o * CHANS : (o + 1) * CHANS, :].reshape(depth, LANES).astype(jnp.float32) for o in range(4)]
     lane = lax.broadcasted_iota(jnp.int32, (depth, LANES), 1)
@@ -161,11 +197,11 @@
 
     @pl.when(part == 0)
     def _():
-        out_ref[...] = total
+        out_ref[:, 0, :] = total
 
     @pl.when(part > 0)
     def _():
-        out_ref[...] += total
+        out_ref[:, 0, :] += total
 
 
 def dedisperse(arrived, dm_trials, chan_total):
@@ -185,8 +221,8 @@
             pl.BlockSpec((1, depth), lambda i: (0, i)),
             pl.BlockSpec((trials, 1), lambda i: (0, 0)),
         ],
-        out_specs=pl.BlockSpec((trials, 2 * LANES), lambda i: (0, 0)),
-        out_shape=jax.ShapeDtypeStruct((trials, 2 * LANES), jnp.float32),
+        out_specs=pl.BlockSpec((trials, 1, 2 * LANES), lambda i: (0, 0, 0)),
+        out_shape=jax.ShapeDtypeStruct((trials, 1, 2 * LANES), jnp.float32),
         scratch_shapes=[
             pltpu.VMEM((trials, (MAXD + 1) * depth), jnp.bfloat16),
             pltpu.VMEM(((MAXD + 1) * depth, 2 * LANES), jnp.bfloat16),
@@ -202,8 +238,7 @@
     outgoing = beams(voltages, scales, feed_positions, beam_directions, chan_total)
     outgoing = outgoing.reshape(groups, 4 * CHANS, LANES)
     arrived = lax.all_to_all(outgoing, "chan", split_axis=0, concat_axis=0, tiled=True)
-    result = dedisperse(arrived, dm_trials, chan_total)
-    return result[:, None, :]
+    return dedisperse(arrived, dm_trials, chan_total)
 
 
 def solution(mesh):

time: 31.6 us -> 27.3 us (0.86)
  local copies, waits for them, and re-layouts: 3.35 us -> 0.14 us
  Pallas kernels: 10.6 us -> 9.58 us
    unnamed x10 -> x4, local copies, waits for them, and re-layouts: 2.24 us -> 0.01 us
    pallas_call x1, Pallas kernels: 9.44 us -> 7.87 us  [beams(): pl.pallas_call(functools.partial(beam_kernel, chan_total, blocks), grid=(...]
    broadcast_in_dim x1 -> x0, local copies, waits for them, and re-layouts: 0.97 us -> none  [local(): return result[:, None, :]]
    pallas_call x1, Pallas kernels: 1.13 us -> 1.71 us  [dedisperse(): pl.pallas_call(functools.partial(dedisperse_kernel, scaling, divisor), gr...]
where the time goes in v2:
time: 27.3 us; the launch traced here: 27.1 us
  waiting for transfers between devices  9.9 us (36%)
  Pallas kernels  9.58 us (35%)
  starting transfers between devices  7.4 us (27%)
    all_to_all x1, waiting for transfers between devices, local(): lax.all_to_all(outgoing, 'chan', split_axis=0, concat_axis=0, tiled=True)  9.9 us
    pallas_call x1, Pallas kernels, beams(): pl.pallas_call(functools.partial(beam_kernel, chan_total, blocks), grid=(...  7.87 us
    all_to_all x1, starting transfers between devices, local(): lax.all_to_all(outgoing, 'chan', split_axis=0, concat_axis=0, tiled=True)  7.4 us
    pallas_call x1, Pallas kernels, dedisperse(): pl.pallas_call(functools.partial(dedisperse_kernel, scaling, divisor), gr...  1.71 us
  transfers between devices with their start and end apart: 1, of which 1 were waited for; matrix products, arithmetic and copies ran while one was open for 0% of the time, Pallas kernels for 0%

profile of v2, /device:TPU:0, one launch (start us, length us, event | category | flops | bytes accessed | tf_op | source)
XLA Modules:
  0.0 27.1 jit_solution(13700761136153231331)
XLA Ops:
  0.0 0.0 copy-start
  0.0 0.0 copy-start.1
  0.0 7.9 %beams.1 = bf16[2,8,64,128]{3,2,1,0:T(8,128)(2,1)} custom-call(s32[16,2,2,32,1024]{4,3,2,1,0:T(8,128)} %volt_hbm.1, s32[16,1024]{1,0:T(8,128)} %scales_hbm.1, f32[3,1024]{1,0:T(4,128)} %pos_hbm.1, f32[3,128]{1,0:T(4,128)} %dirs_hbm.1), custom_call_target="tpu_custom_call" | custom-call | tf_op jit(solution)/shard_map/beams/pallas_call | solution.py:149
  7.9 7.4 %all-to-all-start = ((bf16[16,64,128]{2,1,0:T(8,128)(2,1)}), bf16[16,64,128]{2,1,0:T(8,128)(2,1)S(1)}, u32[]{:S(2)}, u32[]{:S(2)}) async-start(bf16[16,64,128]{2,1,0:T(8,128)(2,1)} %bitcast), calls=%async_computation | async-start | bytes 524288 | tf_op jit(solution)/shard_map/all_to_all | solution.py:240
  15.3 0.0 copy-done.1
  15.3 0.1 copy.7.dm_ref
  15.4 9.9 %all-to-all-done.arrived_ref = bf16[16,64,128]{2,1,0:T(8,128)(2,1)S(1)} async-done(((bf16[16,64,128]{2,1,0:T(8,128)(2,1)}), bf16[16,64,128]{2,1,0:T(8,128)(2,1)S(1)}, u32[]{:S(2)}, u32[]{:S(2)}) %all-to-all-start) | async-done | bytes 262176 | tf_op jit(solution)/shard_map/all_to_all | solution.py:240
  25.3 0.0 copy-done
  25.3 1.7 %dedisperse.1 = f32[256,1,256]{2,1,0:T(1,128)} custom-call(bf16[16,64,128]{2,1,0:T(8,128)(2,1)S(1)} %all-to-all-done.arrived_ref, s32[1,256]{1,0:T(1,128)S(1)} %copy-done, s32[256,1]{1,0:T(8,128)S(1)} %copy.7.dm_ref), custom_call_target="tpu_custom_call" | custom-call | tf_op jit(solution)/shard_map/dedisperse/pallas_call | solution.py:216
Async XLA Ops:
  0.0 25.3 %copy-start = (s32[1,256]{1,0:T(1,128)S(1)}, s32[1,256]{1,0:T(1,128)}, u32[]{:S(2)}) copy-start(s32[1,256]{1,0:T(1,128)} %constant.5.sweeps_ref) | copy-start | bytes 3076
  0.0 15.3 %copy-start.1 = (s32[256]{0:T(256)S(1)}, s32[256]{0:T(256)}, u32[]{:S(2)}) copy-start(s32[256]{0:T(256)} %param.10) | copy-start | bytes 3076
  7.9 17.5 %all-to-all-start = ((bf16[16,64,128]{2,1,0:T(8,128)(2,1)}), bf16[16,64,128]{2,1,0:T(8,128)(2,1)S(1)}, u32[]{:S(2)}, u32[]{:S(2)}) async-start(bf16[16,64,128]{2,1,0:T(8,128)(2,1)} %bitcast), calls=%async_computation | async-start | bytes 524288 | tf_op jit(solution)/shard_map/all_to_all | solution.py:240

commit v3 on v2

--- a/solution.py
+++ b/solution.py
@@ -15,8 +15,9 @@
 LANES = 128
 CHANS = 16
 OCTET = 8
-BATCHES = (4, 4, 4, 4)
+BATCHES = (5, 6, 5)
 DEPTH = 256
+EARLY = 1
 BEAM_VMEM = 40 * 1024 * 1024
 VMEM_LIMIT = 24 * 1024 * 1024
 
@@ -82,7 +83,7 @@
     return total
 
 
-def beam_kernel(chan_total, blocks, volt_hbm, scales_hbm, pos_hbm, dirs_hbm, out_ref, volt, scales, pos, dirs, cosine, sine, power, sems, small_sems):
+def beam_kernel(chan_total, blocks, volt_hbm, scales_hbm, pos_hbm, dirs_hbm, out_hbm, volt, scales, pos, dirs, cosine, sine, power, stage, sems, small_sems, out_sems):
     edges = [sum(BATCHES[:k]) for k in range(len(BATCHES) + 1)]
     small = [
         pltpu.make_async_copy(source, target, small_sems.at[k])
@@ -93,14 +94,28 @@
         for k, (low, high) in enumerate(zip(edges, edges[1:]))
     ]
 
+    first_row = 0 if blocks == 1 else pl.program_id(0) * OCTET
+
+    def leave(source, group, octet):
+        target = out_hbm.at[group, pl.ds(first_row, OCTET), octet * CHANS : (octet + 1) * CHANS, :]
+        return pltpu.make_async_copy(source, target, out_sems.at[4 * group + octet])
+
+    leaving = [[leave(stage.at[octet], 0, octet)] for octet in range(4)]
+    for octet in range(2):
+        leaving[2 + octet].append(leave(stage.at[2 + octet], 1, octet))
+        leaving[octet].append(leave(stage.at[4], 1, 2 + octet))
+
     def start_all():
-        for copy in small + copies:
+        for copy in small + copies[:EARLY]:
             copy.start()
         for copy in small:
             copy.wait()
+        for copy in copies[EARLY:]:
+            copy.start()
 
     in_first_block(blocks, start_all)
 
+    stage[4] = jnp.zeros((OCTET, CHANS, LANES), jnp.bfloat16)
     first_chan = lax.axis_index("chan") * CHANS
     frequency = first_chan.astype(jnp.float32) / chan_total + 1.0
     feeds = pos.shape[1]
@@ -129,17 +144,15 @@
         flat = detected - jnp.mean(detected, axis=0, keepdims=True)
         power[pl.ds(c, window, stride=CHANS), :] = flat
 
-    zeros = jnp.zeros((2 * CHANS, LANES), jnp.bfloat16)
     for octet in range(window // OCTET):
         tiles = [power[(octet * OCTET + t) * CHANS : (octet * OCTET + t + 1) * CHANS, :] for t in range(OCTET)]
-        tiles = swap_lanes_and_list(tiles, CHANS)
+        tiles = swap_lanes_and_list([tile.astype(jnp.bfloat16) for tile in tiles], CHANS)
         for h in range(OCTET):
-            tile = tiles[h].astype(jnp.bfloat16)
-            out_ref[0, h, octet * CHANS : (octet + 1) * CHANS, :] = tile
-            if octet >= 2:
-                out_ref[1, h, (octet - 2) * CHANS : (octet - 1) * CHANS, :] = tile
-    for h in range(OCTET):
-        out_ref[1, h, 2 * CHANS :, :] = zeros
+            stage[octet, h] = tiles[h]
+        for copy in leaving[octet]:
+            copy.start()
+    for copy in sum(leaving, []):
+        copy.wait()
 
 
 def beams(voltages, scales, feed_positions, beam_directions, chan_total):
@@ -155,7 +168,7 @@
             pl.BlockSpec(memory_space=pl.ANY),
             pl.BlockSpec(memory_space=pl.ANY),
         ],
-        out_specs=pl.BlockSpec((2, OCTET, 4 * CHANS, LANES), lambda i: (0, i, 0, 0)),
+        out_specs=pl.BlockSpec(memory_space=pl.ANY),
         out_shape=jax.ShapeDtypeStruct((2, blocks * OCTET, 4 * CHANS, LANES), jnp.bfloat16),
         scratch_shapes=[
             pltpu.VMEM(voltages.shape, jnp.int32),
@@ -165,21 +178,46 @@
             pltpu.VMEM((feeds, LANES), jnp.float32),
             pltpu.VMEM((feeds, LANES), jnp.float32),
             pltpu.VMEM((window * CHANS, LANES), jnp.float32),
+            pltpu.VMEM((5, OCTET, CHANS, LANES), jnp.bfloat16),
             pltpu.SemaphoreType.DMA((len(BATCHES),)),
             pltpu.SemaphoreType.DMA((3,)),
+            pltpu.SemaphoreType.DMA((8,)),
         ],
         compiler_params=pltpu.CompilerParams(vmem_limit_bytes=BEAM_VMEM),
         name="beams",
     )(*(pltpu.with_memory_space_constraint(x, pltpu.HBM) for x in (voltages, scales, feed_positions, beam_directions)))
 
 
-def dedisperse_kernel(scaling, divisor, arrived_ref, sweeps_ref, dm_ref, out_ref, masks, pieces):
-    trials = out_ref.shape[0]
-    part = pl.program_id(0)
+def masks_kernel(divisor, sweeps_ref, dm_ref, masks_ref):
     product = (dm_ref[...] * sweeps_ref[...]).astype(jnp.float32)
     delays = jnp.floor((product + 0.5) * (1.0 / divisor))
     depth = delays.shape[1]
-    tiles = [arrived_ref[:, o * CHANS : (o + 1) * CHANS, :].reshape(depth, LANES).astype(jnp.float32) for o in range(4)]
+    for shift in range(MAXD + 1):
+        masks_ref[:, shift * depth : (shift + 1) * depth] = jnp.where(delays == shift, 1.0, 0.0).astype(jnp.bfloat16)
+
+
+def shift_masks(dm_trials, chan_total, depth):
+    trials = dm_trials.shape[0]
+    ids = np.arange(chan_total, dtype=np.int64)
+    sweeps = ((256 * chan_total * chan_total) // ((chan_total + ids) ** 2) - 64).astype(np.int32)
+    return pl.pallas_call(
+        functools.partial(masks_kernel, trials * 192 // (MAXD + 1)),
+        grid=(chan_total // depth,),
+        in_specs=[
+            pl.BlockSpec((1, depth), lambda i: (0, i)),
+            pl.BlockSpec((trials, 1), lambda i: (0, 0)),
+        ],
+        out_specs=pl.BlockSpec((trials, (MAXD + 1) * depth), lambda i: (0, i)),
+        out_shape=jax.ShapeDtypeStruct((trials, (MAXD + 1) * chan_total), jnp.bfloat16),
+        compiler_params=pltpu.CompilerParams(vmem_limit_bytes=VMEM_LIMIT),
+        name="shift_masks",
+    )(jnp.asarray(sweeps)[None, :], dm_trials[:, None])
+
+
+def dedisperse_kernel(scaling, parts, arrived_ref, masks_ref, out_hbm, pieces, total, sem):
+    part = pl.program_id(0)
+    depth = arrived_ref.shape[0] * CHANS
+    tiles = [arrived_ref[:, o * CHANS : (o + 1) * CHANS, :].reshape(depth, LANES) for o in range(4)]
     lane = lax.broadcasted_iota(jnp.int32, (depth, LANES), 1)
     for r in range(OCTET):
         if r == 0:
@@ -187,49 +225,50 @@
         else:
             rolled = [pltpu.roll(tile, LANES - r * CHANS, 1) for tile in tiles]
             moved = [jnp.where(lane < LANES - r * CHANS, rolled[o], rolled[o + 1]) for o in range(3)]
-        moved = [tile.astype(jnp.bfloat16) for tile in moved]
         for a in range(2):
             shift = OCTET * a + r
-            masks[:, shift * depth : (shift + 1) * depth] = jnp.where(delays == shift, 1.0, 0.0).astype(jnp.bfloat16)
             pieces[shift * depth : (shift + 1) * depth, :LANES] = moved[a]
             pieces[shift * depth : (shift + 1) * depth, LANES:] = moved[a + 1]
-    total = jnp.dot(masks[...], pieces[...], preferred_element_type=jnp.float32) * scaling
-
-    @pl.when(part == 0)
-    def _():
-        out_ref[:, 0, :] = total
-
-    @pl.when(part > 0)
-    def _():
-        out_ref[:, 0, :] += total
-
-
-def dedisperse(arrived, dm_trials, chan_total):
+    summed = jnp.dot(masks_ref[...], pieces[...], preferred_element_type=jnp.float32) * scaling
+    if parts == 1:
+        total[...] = summed
+    else:
+        total[...] = jnp.where(part == 0, 0.0, total[...]) + summed
+
+    def leave():
+        copy = pltpu.make_async_copy(total, out_hbm.at[:, 0, :], sem)
+        copy.start()
+        copy.wait()
+
+    if parts == 1:
+        leave()
+    else:
+        pl.when(part == parts - 1)(leave)
+
+
+def dedisperse(arrived, masks, chan_total):
     sources = arrived.shape[0]
-    trials = dm_trials.shape[0]
-    ids = np.arange(chan_total, dtype=np.int64)
-    sweeps = ((256 * chan_total * chan_total) // ((chan_total + ids) ** 2) - 64).astype(np.int32)
+    trials = masks.shape[0]
     group = min(sources, 16)
     depth = group * CHANS
     scaling = POWER_SCALE / math.sqrt(chan_total)
-    divisor = trials * 192 // (MAXD + 1)
     return pl.pallas_call(
-        functools.partial(dedisperse_kernel, scaling, divisor),
+        functools.partial(dedisperse_kernel, scaling, sources // group),
         grid=(sources // group,),
         in_specs=[
             pl.BlockSpec((group, 4 * CHANS, LANES), lambda i: (i, 0, 0)),
-            pl.BlockSpec((1, depth), lambda i: (0, i)),
-            pl.BlockSpec((trials, 1), lambda i: (0, 0)),
-        ],
-        out_specs=pl.BlockSpec((trials, 1, 2 * LANES), lambda i: (0, 0, 0)),
+            pl.BlockSpec((trials, (MAXD + 1) * depth), lambda i: (0, i)),
+        ],
+        out_specs=pl.BlockSpec(memory_space=pl.ANY),
         out_shape=jax.ShapeDtypeStruct((trials, 1, 2 * LANES), jnp.float32),
         scratch_shapes=[
-            pltpu.VMEM((trials, (MAXD + 1) * depth), jnp.bfloat16),
             pltpu.VMEM(((MAXD + 1) * depth, 2 * LANES), jnp.bfloat16),
+            pltpu.VMEM((trials, 2 * LANES), jnp.float32),
+            pltpu.SemaphoreType.DMA(()),
         ],
         compiler_params=pltpu.CompilerParams(vmem_limit_bytes=VMEM_LIMIT),
         name="dedisperse",
-    )(arrived, jnp.asarray(sweeps)[None, :], dm_trials[:, None])
+    )(arrived, masks)
 
 
 def local(voltages, scales, feed_positions, beam_directions, dm_trials):
@@ -238,7 +277,8 @@
     outgoing = beams(voltages, scales, feed_positions, beam_directions, chan_total)
     outgoing = outgoing.reshape(groups, 4 * CHANS, LANES)
     arrived = lax.all_to_all(outgoing, "chan", split_axis=0, concat_axis=0, tiled=True)
-    return dedisperse(arrived, dm_trials, chan_total)
+    masks = shift_masks(dm_trials, chan_total, min(groups, 16) * CHANS)
+    return dedisperse(arrived, masks, chan_total)
 
 
 def solution(mesh):

time: 27.3 us -> 25.2 us (0.923)
  Pallas kernels: 9.58 us -> 7.96 us
  waiting for transfers between devices: 9.9 us -> 9.43 us
    pallas_call x1, Pallas kernels: 7.87 us -> 5.84 us  [beams(): pl.pallas_call(functools.partial(beam_kernel, chan_total, blocks), grid=(...]
    all_to_all x1, waiting for transfers between devices: 9.9 us -> 9.43 us  [local(): lax.all_to_all(outgoing, 'chan', split_axis=0, concat_axis=0, tiled=True)]
    pallas_call x1 -> x2, Pallas kernels: 1.71 us -> 2.11 us  [the longest x1 1.66 us: dedisperse(): pl.pallas_call(functools.partial(dedisperse_kernel, scaling, sources // g...]
  transfers between devices with their start and end apart: 1 -> 1, of which waited for: 1 -> 1; matrix products, arithmetic and copies ran while one was open for 0% -> 1% of each run, Pallas kernels for 0% -> 2%
where the time goes in v3:
time: 25.2 us; the launch traced here: 25 us
  waiting for transfers between devices  9.43 us (37%)
  Pallas kernels  7.96 us (32%)
  starting transfers between devices  7.4 us (29%)
    all_to_all x1, waiting for transfers between devices, local(): lax.all_to_all(outgoing, 'chan', split_axis=0, concat_axis=0, tiled=True)  9.43 us
    all_to_all x1, starting transfers between devices, local(): lax.all_to_all(outgoing, 'chan', split_axis=0, concat_axis=0, tiled=True)  7.4 us
    pallas_call x1, Pallas kernels, beams(): pl.pallas_call(functools.partial(beam_kernel, chan_total, blocks), grid=(...  5.84 us
    pallas_call x1, Pallas kernels, dedisperse(): pl.pallas_call(functools.partial(dedisperse_kernel, scaling, sources // g...  1.66 us
  transfers between devices with their start and end apart: 1, of which 1 were waited for; matrix products, arithmetic and copies ran while one was open for 1% of the time, Pallas kernels for 2%

profile of v3, /device:TPU:0, one launch (start us, length us, event | category | flops | bytes accessed | tf_op | source)
XLA Modules:
  0.0 25.0 jit_solution(7624446776369601767)
XLA Ops:
  0.0 0.0 copy-start
  0.0 0.0 copy-start.1
  0.0 5.8 %beams.1 = bf16[2,8,64,128]{3,2,1,0:T(8,128)(2,1)} custom-call(s32[16,2,2,32,1024]{4,3,2,1,0:T(8,128)} %volt_hbm.1, s32[16,1024]{1,0:T(8,128)} %scales_hbm.1, f32[3,1024]{1,0:T(4,128)} %pos_hbm.1, f32[3,128]{1,0:T(4,128)} %dirs_hbm.1), custom_call_target="tpu_custom_call" | custom-call | tf_op jit(solution)/shard_map/beams/pallas_call | solution.py:162
  5.9 7.4 %all-to-all-start = ((bf16[16,64,128]{2,1,0:T(8,128)(2,1)}), bf16[16,64,128]{2,1,0:T(8,128)(2,1)S(1)}, u32[]{:S(2)}, u32[]{:S(2)}) async-start(bf16[16,64,128]{2,1,0:T(8,128)(2,1)} %bitcast), calls=%async_computation | async-start | bytes 524288 | tf_op jit(solution)/shard_map/all_to_all | solution.py:279
  13.3 0.0 copy-done.1
  13.3 0.1 copy.7.dm_ref
  13.4 0.0 copy-done
  13.4 0.4 %shift_masks.1.masks_ref = bf16[256,4096]{1,0:T(8,128)(2,1)S(1)} custom-call(s32[1,256]{1,0:T(1,128)S(1)} %copy-done, s32[256,1]{1,0:T(8,128)S(1)} %copy.7.dm_ref), custom_call_target="tpu_custom_call" | custom-call | tf_op jit(solution)/shard_map/shift_masks/pallas_call | solution.py:203
  13.9 9.4 %all-to-all-done.arrived_ref = bf16[16,64,128]{2,1,0:T(8,128)(2,1)S(1)} async-done(((bf16[16,64,128]{2,1,0:T(8,128)(2,1)}), bf16[16,64,128]{2,1,0:T(8,128)(2,1)S(1)}, u32[]{:S(2)}, u32[]{:S(2)}) %all-to-all-start) | async-done | bytes 262176 | tf_op jit(solution)/shard_map/all_to_all | solution.py:279
  23.3 1.7 %dedisperse.1 = f32[256,1,256]{2,1,0:T(1,128)} custom-call(bf16[16,64,128]{2,1,0:T(8,128)(2,1)S(1)} %all-to-all-done.arrived_ref, bf16[256,4096]{1,0:T(8,128)(2,1)S(1)} %shift_masks.1.masks_ref), custom_call_target="tpu_custom_call" | custom-call | tf_op jit(solution)/shard_map/dedisperse/pallas_call | solution.py:255
Async XLA Ops:
  0.0 13.4 %copy-start = (s32[1,256]{1,0:T(1,128)S(1)}, s32[1,256]{1,0:T(1,128)}, u32[]{:S(2)}) copy-start(s32[1,256]{1,0:T(1,128)} %constant.5.sweeps_ref) | copy-start | bytes 3076
  0.0 13.3 %copy-start.1 = (s32[256]{0:T(256)S(1)}, s32[256]{0:T(256)}, u32[]{:S(2)}) copy-start(s32[256]{0:T(256)} %param.10) | copy-start | bytes 3076
  5.9 17.5 %all-to-all-start = ((bf16[16,64,128]{2,1,0:T(8,128)(2,1)}), bf16[16,64,128]{2,1,0:T(8,128)(2,1)S(1)}, u32[]{:S(2)}, u32[]{:S(2)}) async-start(bf16[16,64,128]{2,1,0:T(8,128)(2,1)} %bitcast), calls=%async_computation | async-start | bytes 524288 | tf_op jit(solution)/shard_map/all_to_all | solution.py:279

commit v4 on v3

--- a/solution.py
+++ b/solution.py
@@ -1,7 +1,5 @@
 import functools
 import math
-
-import numpy as np
 
 import jax
 import jax.numpy as jnp
@@ -83,27 +81,24 @@
     return total
 
 
-def beam_kernel(chan_total, blocks, volt_hbm, scales_hbm, pos_hbm, dirs_hbm, out_hbm, volt, scales, pos, dirs, cosine, sine, power, stage, sems, small_sems, out_sems):
+def write_delays(divisor, dm, delays_ref):
+    trials, chan_total = delays_ref.shape
+    upper = chan_total + lax.broadcasted_iota(jnp.int32, (1, chan_total), 1)
+    sweeps = ((256 * chan_total * chan_total) // (upper * upper) - 64).astype(jnp.float32)
+    column = jnp.transpose(jnp.broadcast_to(dm[...].astype(jnp.float32), (8, trials)))[:, 0:1]
+    delays_ref[...] = jnp.floor((column * sweeps + 0.5) * (1.0 / divisor))
+
+
+def beam_kernel(chan_total, blocks, divisor, volt_hbm, scales_hbm, pos_hbm, dirs_hbm, dm_hbm, out_ref, delays_ref, volt, scales, pos, dirs, dm, cosine, sine, power, sems, small_sems):
     edges = [sum(BATCHES[:k]) for k in range(len(BATCHES) + 1)]
     small = [
         pltpu.make_async_copy(source, target, small_sems.at[k])
-        for k, (source, target) in enumerate(((pos_hbm, pos), (dirs_hbm, dirs), (scales_hbm, scales)))
+        for k, (source, target) in enumerate(((pos_hbm, pos), (dirs_hbm, dirs), (scales_hbm, scales), (dm_hbm, dm)))
     ]
     copies = [
         pltpu.make_async_copy(volt_hbm.at[low:high], volt.at[low:high], sems.at[k])
         for k, (low, high) in enumerate(zip(edges, edges[1:]))
     ]
-
-    first_row = 0 if blocks == 1 else pl.program_id(0) * OCTET
-
-    def leave(source, group, octet):
-        target = out_hbm.at[group, pl.ds(first_row, OCTET), octet * CHANS : (octet + 1) * CHANS, :]
-        return pltpu.make_async_copy(source, target, out_sems.at[4 * group + octet])
-
-    leaving = [[leave(stage.at[octet], 0, octet)] for octet in range(4)]
-    for octet in range(2):
-        leaving[2 + octet].append(leave(stage.at[2 + octet], 1, octet))
-        leaving[octet].append(leave(stage.at[4], 1, 2 + octet))
 
     def start_all():
         for copy in small + copies[:EARLY]:
@@ -115,7 +110,7 @@
 
     in_first_block(blocks, start_all)
 
-    stage[4] = jnp.zeros((OCTET, CHANS, LANES), jnp.bfloat16)
+    in_first_block(blocks, lambda: write_delays(divisor, dm, delays_ref))
     first_chan = lax.axis_index("chan") * CHANS
     frequency = first_chan.astype(jnp.float32) / chan_total + 1.0
     feeds = pos.shape[1]
@@ -148,77 +143,56 @@
         tiles = [power[(octet * OCTET + t) * CHANS : (octet * OCTET + t + 1) * CHANS, :] for t in range(OCTET)]
         tiles = swap_lanes_and_list([tile.astype(jnp.bfloat16) for tile in tiles], CHANS)
         for h in range(OCTET):
-            stage[octet, h] = tiles[h]
-        for copy in leaving[octet]:
-            copy.start()
-    for copy in sum(leaving, []):
-        copy.wait()
-
-
-def beams(voltages, scales, feed_positions, beam_directions, chan_total):
+            out_ref[0, h, octet * CHANS : (octet + 1) * CHANS, :] = tiles[h]
+            if octet >= 2:
+                out_ref[1, h, (octet - 2) * CHANS : (octet - 1) * CHANS, :] = tiles[h]
+    for h in range(OCTET):
+        out_ref[1, h, 2 * CHANS :, :] = jnp.zeros((2 * CHANS, LANES), jnp.bfloat16)
+
+
+def beams(voltages, scales, feed_positions, beam_directions, dm_trials, chan_total):
     window, feeds = voltages.shape[3:]
     beam_count = beam_directions.shape[1]
     blocks = beam_count // LANES
+    trials = dm_trials.shape[0]
+    divisor = trials * 192 // (MAXD + 1)
+    inputs = (voltages, scales, feed_positions, beam_directions, dm_trials[None, :])
     return pl.pallas_call(
-        functools.partial(beam_kernel, chan_total, blocks),
+        functools.partial(beam_kernel, chan_total, blocks, divisor),
         grid=(blocks,),
-        in_specs=[
-            pl.BlockSpec(memory_space=pl.ANY),
-            pl.BlockSpec(memory_space=pl.ANY),
-            pl.BlockSpec(memory_space=pl.ANY),
-            pl.BlockSpec(memory_space=pl.ANY),
-        ],
-        out_specs=pl.BlockSpec(memory_space=pl.ANY),
-        out_shape=jax.ShapeDtypeStruct((2, blocks * OCTET, 4 * CHANS, LANES), jnp.bfloat16),
+        in_specs=[pl.BlockSpec(memory_space=pl.ANY)] * len(inputs),
+        out_specs=(
+            pl.BlockSpec((2, OCTET, 4 * CHANS, LANES), lambda i: (0, i, 0, 0)),
+            pl.BlockSpec((trials, chan_total), lambda i: (0, 0)),
+        ),
+        out_shape=(
+            jax.ShapeDtypeStruct((2, blocks * OCTET, 4 * CHANS, LANES), jnp.bfloat16),
+            jax.ShapeDtypeStruct((trials, chan_total), jnp.float32),
+        ),
         scratch_shapes=[
             pltpu.VMEM(voltages.shape, jnp.int32),
             pltpu.VMEM(scales.shape, jnp.int32),
             pltpu.VMEM(feed_positions.shape, jnp.float32),
             pltpu.VMEM(beam_directions.shape, jnp.float32),
+            pltpu.VMEM((1, trials), jnp.int32),
             pltpu.VMEM((feeds, LANES), jnp.float32),
             pltpu.VMEM((feeds, LANES), jnp.float32),
             pltpu.VMEM((window * CHANS, LANES), jnp.float32),
-            pltpu.VMEM((5, OCTET, CHANS, LANES), jnp.bfloat16),
             pltpu.SemaphoreType.DMA((len(BATCHES),)),
-            pltpu.SemaphoreType.DMA((3,)),
-            pltpu.SemaphoreType.DMA((8,)),
+            pltpu.SemaphoreType.DMA((len(inputs) - 1,)),
         ],
         compiler_params=pltpu.CompilerParams(vmem_limit_bytes=BEAM_VMEM),
         name="beams",
-    )(*(pltpu.with_memory_space_constraint(x, pltpu.HBM) for x in (voltages, scales, feed_positions, beam_directions)))
-
-
-def masks_kernel(divisor, sweeps_ref, dm_ref, masks_ref):
-    product = (dm_ref[...] * sweeps_ref[...]).astype(jnp.float32)
-    delays = jnp.floor((product + 0.5) * (1.0 / divisor))
-    depth = delays.shape[1]
-    for shift in range(MAXD + 1):
-        masks_ref[:, shift * depth : (shift + 1) * depth] = jnp.where(delays == shift, 1.0, 0.0).astype(jnp.bfloat16)
-
-
-def shift_masks(dm_trials, chan_total, depth):
-    trials = dm_trials.shape[0]
-    ids = np.arange(chan_total, dtype=np.int64)
-    sweeps = ((256 * chan_total * chan_total) // ((chan_total + ids) ** 2) - 64).astype(np.int32)
-    return pl.pallas_call(
-        functools.partial(masks_kernel, trials * 192 // (MAXD + 1)),
-        grid=(chan_total // depth,),
-        in_specs=[
-            pl.BlockSpec((1, depth), lambda i: (0, i)),
-            pl.BlockSpec((trials, 1), lambda i: (0, 0)),
-        ],
-        out_specs=pl.BlockSpec((trials, (MAXD + 1) * depth), lambda i: (0, i)),
-        out_shape=jax.ShapeDtypeStruct((trials, (MAXD + 1) * chan_total), jnp.bfloat16),
-        compiler_params=pltpu.CompilerParams(vmem_limit_bytes=VMEM_LIMIT),
-        name="shift_masks",
-    )(jnp.asarray(sweeps)[None, :], dm_trials[:, None])
-
-
-def dedisperse_kernel(scaling, parts, arrived_ref, masks_ref, out_hbm, pieces, total, sem):
+    )(*(pltpu.with_memory_space_constraint(x, pltpu.HBM) for x in inputs))
+
+
+def dedisperse_kernel(scaling, parts, arrived_ref, delays_ref, out_hbm, total, sem):
     part = pl.program_id(0)
     depth = arrived_ref.shape[0] * CHANS
+    delays = delays_ref[...]
     tiles = [arrived_ref[:, o * CHANS : (o + 1) * CHANS, :].reshape(depth, LANES) for o in range(4)]
     lane = lax.broadcasted_iota(jnp.int32, (depth, LANES), 1)
+    summed = None
     for r in range(OCTET):
         if r == 0:
             moved = tiles[:3]
@@ -226,10 +200,11 @@
             rolled = [pltpu.roll(tile, LANES - r * CHANS, 1) for tile in tiles]
             moved = [jnp.where(lane < LANES - r * CHANS, rolled[o], rolled[o + 1]) for o in range(3)]
         for a in range(2):
-            shift = OCTET * a + r
-            pieces[shift * depth : (shift + 1) * depth, :LANES] = moved[a]
-            pieces[shift * depth : (shift + 1) * depth, LANES:] = moved[a + 1]
-    summed = jnp.dot(masks_ref[...], pieces[...], preferred_element_type=jnp.float32) * scaling
+            mask = jnp.where(delays == OCTET * a + r, 1.0, 0.0).astype(jnp.bfloat16)
+            piece = jnp.concatenate([moved[a], moved[a + 1]], axis=1)
+            product = jnp.dot(mask, piece, preferred_element_type=jnp.float32)
+            summed = product if summed is None else summed + product
+    summed = summed * scaling
     if parts == 1:
         total[...] = summed
     else:
@@ -246,9 +221,9 @@
         pl.when(part == parts - 1)(leave)
 
 
-def dedisperse(arrived, masks, chan_total):
+def dedisperse(arrived, delays):
     sources = arrived.shape[0]
-    trials = masks.shape[0]
+    trials, chan_total = delays.shape
     group = min(sources, 16)
     depth = group * CHANS
     scaling = POWER_SCALE / math.sqrt(chan_total)
@@ -257,28 +232,26 @@
         grid=(sources // group,),
         in_specs=[
             pl.BlockSpec((group, 4 * CHANS, LANES), lambda i: (i, 0, 0)),
-            pl.BlockSpec((trials, (MAXD + 1) * depth), lambda i: (0, i)),
+            pl.BlockSpec((trials, depth), lambda i: (0, i)),
         ],
         out_specs=pl.BlockSpec(memory_space=pl.ANY),
         out_shape=jax.ShapeDtypeStruct((trials, 1, 2 * LANES), jnp.float32),
         scratch_shapes=[
-            pltpu.VMEM(((MAXD + 1) * depth, 2 * LANES), jnp.bfloat16),
             pltpu.VMEM((trials, 2 * LANES), jnp.float32),
             pltpu.SemaphoreType.DMA(()),
         ],
         compiler_params=pltpu.CompilerParams(vmem_limit_bytes=VMEM_LIMIT),
         name="dedisperse",
-    )(arrived, masks)
+    )(arrived, delays)
 
 
 def local(voltages, scales, feed_positions, beam_directions, dm_trials):
     groups = lax.axis_size("chan")
     chan_total = groups * voltages.shape[0]
-    outgoing = beams(voltages, scales, feed_positions, beam_directions, chan_total)
+    outgoing, delays = beams(voltages, scales, feed_positions, beam_directions, dm_trials, chan_total)
     outgoing = outgoing.reshape(groups, 4 * CHANS, LANES)
     arrived = lax.all_to_all(outgoing, "chan", split_axis=0, concat_axis=0, tiled=True)
-    masks = shift_masks(dm_trials, chan_total, min(groups, 16) * CHANS)
-    return dedisperse(arrived, masks, chan_total)
+    return dedisperse(arrived, delays)
 
 
 def solution(mesh):

time: 25.2 us -> 24.2 us (0.960)
  blocking collectives: 0 us -> 17.2 us
  waiting for transfers between devices: 9.43 us -> 0 us
  starting transfers between devices: 7.4 us -> 0 us
  Pallas kernels: 7.96 us -> 6.72 us
    all_to_all x0 -> x1, blocking collectives: none -> 17.2 us  [local(): lax.all_to_all(outgoing, 'chan', split_axis=0, concat_axis=0, tiled=True)]
    all_to_all x1 -> x0, waiting for transfers between devices: 9.43 us -> none  [local(): lax.all_to_all(outgoing, 'chan', split_axis=0, concat_axis=0, tiled=True)]
    all_to_all x1 -> x0, starting transfers between devices: 7.4 us -> none  [local(): lax.all_to_all(outgoing, 'chan', split_axis=0, concat_axis=0, tiled=True)]
    pallas_call x2 -> x1, Pallas kernels: 6.29 us -> 5.22 us  [beams(): pl.pallas_call(functools.partial(beam_kernel, chan_total, blocks, divisor...]
  transfers between devices with their start and end apart: 1 -> 0, of which waited for: 1 -> 0; matrix products, arithmetic and copies ran while one was open for 1% -> 0% of each run, Pallas kernels for 2% -> 0%
where the time goes in v4:
time: 24.2 us; the launch traced here: 24 us
  blocking collectives  17.2 us (71%)
  Pallas kernels  6.72 us (28%)
    all_to_all x1, blocking collectives, local(): lax.all_to_all(outgoing, 'chan', split_axis=0, concat_axis=0, tiled=True)  17.2 us
    pallas_call x1, Pallas kernels, beams(): pl.pallas_call(functools.partial(beam_kernel, chan_total, blocks, divisor...  5.22 us
    pallas_call x1, Pallas kernels, dedisperse(): pl.pallas_call(functools.partial(dedisperse_kernel, scaling, sources // g...  1.5 us

profile of v4, /device:TPU:0, one launch (start us, length us, event | category | flops | bytes accessed | tf_op | source)
XLA Modules:
  0.0 24.0 jit_solution(7425364116133316112)
XLA Ops:
  0.0 5.2 %beams.1 = (bf16[2,8,64,128]{3,2,1,0:T(8,128)(2,1)S(1)}, f32[256,256]{1,0:T(8,128)S(1)}) custom-call(s32[16,2,2,32,1024]{4,3,2,1,0:T(8,128)} %volt_hbm.1, s32[16,1024]{1,0:T(8,128)} %scales_hbm.1, f32[3,1024]{1,0:T(4,128)} %pos_hbm.1, f32[3,128]{1,0:T(4,128)} %dirs_hbm.1, s32[1,256]{1,0:T(1,128)} %bitcast.3), custom_call_target="tpu_custom_call" | custom-call | tf_op jit(solution)/shard_map/beams/pallas_call | solution.py:160
  5.2 17.2 %all_to_all.5.arrived_ref = bf16[16,64,128]{2,1,0:T(8,128)(2,1)S(1)} all-to-all(bf16[16,64,128]{2,1,0:T(8,128)(2,1)S(1)} %bitcast.2), channel_id=1, replica_groups=mesh['grp'=2,'chan'=16] {'chan'}, dimensions={0} | all-to-all | bytes 524288 | tf_op jit(solution)/shard_map/all_to_all | solution.py:253
  22.5 1.5 %dedisperse.1 = f32[256,1,256]{2,1,0:T(1,128)} custom-call(bf16[16,64,128]{2,1,0:T(8,128)(2,1)S(1)} %all_to_all.5.arrived_ref, f32[256,256]{1,0:T(8,128)S(1)} %get-tuple-element.8.delays_ref), custom_call_target="tpu_custom_call" | custom-call | tf_op jit(solution)/shard_map/dedisperse/pallas_call | solution.py:230

commit v5 on v4

--- a/solution.py
+++ b/solution.py
@@ -15,12 +15,11 @@
 OCTET = 8
 BATCHES = (5, 6, 5)
 DEPTH = 256
-EARLY = 1
 BEAM_VMEM = 40 * 1024 * 1024
 VMEM_LIMIT = 24 * 1024 * 1024
 
-SIN_TERMS = [(-1) ** k * (2 * math.pi) ** (2 * k + 1) / math.factorial(2 * k + 1) for k in range(5)]
-COS_TERMS = [(-1) ** k * (2 * math.pi) ** (2 * k) / math.factorial(2 * k) for k in range(6)]
+SIN_TERMS = (6.283184916, -41.34158923, 81.59994333, -76.61447253, 41.34288235, -12.47124353)
+COS_TERMS = (0.9999999891, -19.7392045, 64.93911746, -85.45013953, 60.16763095, -25.96759925, 6.528658158)
 
 
 def horner(terms, square):
@@ -31,18 +30,9 @@
 
 
 def cos_sin_turns(turns):
-    quarters = jnp.round(turns * 4.0)
-    rest = turns - quarters * 0.25
+    rest = turns - jnp.round(turns)
     square = rest * rest
-    sine = horner(SIN_TERMS, square) * rest
-    cosine = horner(COS_TERMS, square)
-    which = quarters.astype(jnp.int32)
-    swap = (which & 1) == 1
-    base_cos = jnp.where(swap, sine, cosine)
-    base_sin = jnp.where(swap, cosine, sine)
-    cos_out = jnp.where(((which + 1) & 2) == 2, -base_cos, base_cos)
-    sin_out = jnp.where((which & 2) == 2, -base_sin, base_sin)
-    return cos_out, sin_out
+    return horner(COS_TERMS, square), horner(SIN_TERMS, square) * rest
 
 
 def swap_lanes_and_list(tiles, width):
@@ -81,6 +71,15 @@
     return total
 
 
+def three_parts(rows):
+    rest = jnp.concatenate([rows, jnp.zeros((5, rows.shape[1]), jnp.float32)], axis=0)
+    parts = []
+    for _ in range(3):
+        parts.append(rest.astype(jnp.bfloat16).astype(jnp.float32))
+        rest = rest - parts[-1]
+    return parts
+
+
 def write_delays(divisor, dm, delays_ref):
     trials, chan_total = delays_ref.shape
     upper = chan_total + lax.broadcasted_iota(jnp.int32, (1, chan_total), 1)
@@ -101,12 +100,12 @@
     ]
 
     def start_all():
-        for copy in small + copies[:EARLY]:
-            copy.start()
+        for copy in small:
+            copy.start(priority=0)
+        for copy in copies:
+            copy.start(priority=1)
         for copy in small:
             copy.wait()
-        for copy in copies[EARLY:]:
-            copy.start()
 
     in_first_block(blocks, start_all)
 
@@ -114,15 +113,16 @@
     first_chan = lax.axis_index("chan") * CHANS
     frequency = first_chan.astype(jnp.float32) / chan_total + 1.0
     feeds = pos.shape[1]
-    places = jnp.transpose(jnp.concatenate([pos[...], jnp.zeros((5, feeds), jnp.float32)], axis=0))
     if blocks == 1:
         beam_rows = dirs[...]
     else:
         beam_rows = dirs[:, pl.ds(pl.multiple_of(pl.program_id(0) * LANES, LANES), LANES)]
-    geometry = places[:, 0:1] * beam_rows[0:1, :]
-    geometry = geometry + places[:, 1:2] * beam_rows[1:2, :]
-    geometry = geometry + places[:, 2:3] * beam_rows[2:3, :]
-    cosine[...], sine[...] = cos_sin_turns(frequency * geometry)
+    beam_rows = frequency * beam_rows
+    place_parts, beam_parts = three_parts(pos[...]), three_parts(beam_rows)
+    left = jnp.concatenate([part for part in place_parts for _ in range(3)] + [jnp.zeros((8, feeds), jnp.float32)], axis=0)
+    right = jnp.concatenate(beam_parts * 3 + [jnp.zeros((8, LANES), jnp.float32)], axis=0)
+    turns = lax.dot_general(left.astype(jnp.bfloat16), right.astype(jnp.bfloat16), (((0,), (0,)), ((), ())), preferred_element_type=jnp.float32)
+    cosine[...], sine[...] = cos_sin_turns(turns)
     scale_columns = jnp.transpose(scales[...].astype(jnp.float32)).astype(jnp.bfloat16)
 
     window = volt.shape[3]

time: 24.2 us -> 24 us (level)
  no operation moved by 1% of the time
where the time goes in v5:
time: 24 us; the launch traced here: 23.7 us
  blocking collectives  17.2 us (72%)
  Pallas kernels  6.48 us (27%)
    all_to_all x1, blocking collectives, local(): lax.all_to_all(outgoing, 'chan', split_axis=0, concat_axis=0, tiled=True)  17.2 us
    pallas_call x1, Pallas kernels, beams(): pl.pallas_call(functools.partial(beam_kernel, chan_total, blocks, divisor...  4.98 us
    pallas_call x1, Pallas kernels, dedisperse(): pl.pallas_call(functools.partial(dedisperse_kernel, scaling, sources // g...  1.5 us

profile of v5, /device:TPU:0, one launch (start us, length us, event | category | flops | bytes accessed | tf_op | source)
XLA Modules:
  0.0 23.7 jit_solution(8091688837367381034)
XLA Ops:
  0.0 5.0 %beams.1 = (bf16[2,8,64,128]{3,2,1,0:T(8,128)(2,1)S(1)}, f32[256,256]{1,0:T(8,128)S(1)}) custom-call(s32[16,2,2,32,1024]{4,3,2,1,0:T(8,128)} %volt_hbm.1, s32[16,1024]{1,0:T(8,128)} %scales_hbm.1, f32[3,1024]{1,0:T(4,128)} %pos_hbm.1, f32[3,128]{1,0:T(4,128)} %dirs_hbm.1, s32[1,256]{1,0:T(1,128)} %bitcast.3), custom_call_target="tpu_custom_call" | custom-call | tf_op jit(solution)/shard_map/beams/pallas_call | solution.py:160
  5.0 17.2 %all_to_all.5.arrived_ref = bf16[16,64,128]{2,1,0:T(8,128)(2,1)S(1)} all-to-all(bf16[16,64,128]{2,1,0:T(8,128)(2,1)S(1)} %bitcast.2), channel_id=1, replica_groups=mesh['grp'=2,'chan'=16] {'chan'}, dimensions={0} | all-to-all | bytes 524288 | tf_op jit(solution)/shard_map/all_to_all | solution.py:253
  22.2 1.5 %dedisperse.1 = f32[256,1,256]{2,1,0:T(1,128)} custom-call(bf16[16,64,128]{2,1,0:T(8,128)(2,1)S(1)} %all_to_all.5.arrived_ref, f32[256,256]{1,0:T(8,128)S(1)} %get-tuple-element.8.delays_ref), custom_call_target="tpu_custom_call" | custom-call | tf_op jit(solution)/shard_map/dedisperse/pallas_call | solution.py:230

commit v6 on v5

--- a/solution.py
+++ b/solution.py
@@ -13,8 +13,8 @@
 LANES = 128
 CHANS = 16
 OCTET = 8
-BATCHES = (5, 6, 5)
-DEPTH = 256
+BATCHES = (4, 4, 4, 4)
+DEPTH = 1024
 BEAM_VMEM = 40 * 1024 * 1024
 VMEM_LIMIT = 24 * 1024 * 1024
 
@@ -52,6 +52,16 @@
     return tiles
 
 
+def keep_power(c, product, power, window):
+    half = 2 * window
+    real = product[:half, :LANES] - product[half:, LANES:]
+    imag = product[:half, LANES:] + product[half:, :LANES]
+    both = real * real + imag * imag
+    detected = both[:window] + both[window:]
+    flat = detected - jnp.mean(detected, axis=0, keepdims=True)
+    power[pl.ds(c, window, stride=CHANS), :] = flat
+
+
 def in_first_block(blocks, action):
     if blocks == 1:
         action()
@@ -126,18 +136,16 @@
     scale_columns = jnp.transpose(scales[...].astype(jnp.float32)).astype(jnp.bfloat16)
 
     window = volt.shape[3]
+    held = None
     for c in range(CHANS):
         if c in edges:
             in_first_block(blocks, copies[edges.index(c)].wait)
 
         product = channel_product(volt, c, scale_columns, cosine, sine, window, feeds)
-        half = 2 * window
-        real = product[:half, :LANES] - product[half:, LANES:]
-        imag = product[:half, LANES:] + product[half:, :LANES]
-        both = real * real + imag * imag
-        detected = both[:window] + both[window:]
-        flat = detected - jnp.mean(detected, axis=0, keepdims=True)
-        power[pl.ds(c, window, stride=CHANS), :] = flat
+        if held is not None:
+            keep_power(c - 1, held, power, window)
+        held = product
+    keep_power(CHANS - 1, held, power, window)
 
     for octet in range(window // OCTET):
         tiles = [power[(octet * OCTET + t) * CHANS : (octet * OCTET + t + 1) * CHANS, :] for t in range(OCTET)]

time: 24 us -> 23.9 us (level)
  no operation moved by 1% of the time
where the time goes in v6:
time: 23.9 us; the launch traced here: 23.6 us
  blocking collectives  17.2 us (72%)
  Pallas kernels  6.38 us (27%)
    all_to_all x1, blocking collectives, local(): lax.all_to_all(outgoing, 'chan', split_axis=0, concat_axis=0, tiled=True)  17.2 us
    pallas_call x1, Pallas kernels, beams(): pl.pallas_call(functools.partial(beam_kernel, chan_total, blocks, divisor...  4.88 us
    pallas_call x1, Pallas kernels, dedisperse(): pl.pallas_call(functools.partial(dedisperse_kernel, scaling, sources // g...  1.5 us

profile of v6, /device:TPU:0, one launch (start us, length us, event | category | flops | bytes accessed | tf_op | source)
XLA Modules:
  0.0 23.6 jit_solution(6095845140303491879)
XLA Ops:
  0.0 4.9 %beams.1 = (bf16[2,8,64,128]{3,2,1,0:T(8,128)(2,1)S(1)}, f32[256,256]{1,0:T(8,128)S(1)}) custom-call(s32[16,2,2,32,1024]{4,3,2,1,0:T(8,128)} %volt_hbm.1, s32[16,1024]{1,0:T(8,128)} %scales_hbm.1, f32[3,1024]{1,0:T(4,128)} %pos_hbm.1, f32[3,128]{1,0:T(4,128)} %dirs_hbm.1, s32[1,256]{1,0:T(1,128)} %bitcast.3), custom_call_target="tpu_custom_call" | custom-call | tf_op jit(solution)/shard_map/beams/pallas_call | solution.py:168
  4.9 17.2 %all_to_all.5.arrived_ref = bf16[16,64,128]{2,1,0:T(8,128)(2,1)S(1)} all-to-all(bf16[16,64,128]{2,1,0:T(8,128)(2,1)S(1)} %bitcast.2), channel_id=1, replica_groups=mesh['grp'=2,'chan'=16] {'chan'}, dimensions={0} | all-to-all | bytes 524288 | tf_op jit(solution)/shard_map/all_to_all | solution.py:261
  22.1 1.5 %dedisperse.1 = f32[256,1,256]{2,1,0:T(1,128)} custom-call(bf16[16,64,128]{2,1,0:T(8,128)(2,1)S(1)} %all_to_all.5.arrived_ref, f32[256,256]{1,0:T(8,128)S(1)} %get-tuple-element.8.delays_ref), custom_call_target="tpu_custom_call" | custom-call | tf_op jit(solution)/shard_map/dedisperse/pallas_call | solution.py:238

commit v7 on v6

--- a/solution.py
+++ b/solution.py
@@ -73,7 +73,7 @@
     total = None
     for low in range(0, feeds, DEPTH):
         at = slice(low, low + DEPTH)
-        rows = volt[c, :, :, :, at].reshape(4 * window, DEPTH).astype(jnp.float32).astype(jnp.bfloat16)
+        rows = volt[c, :, :, :, at].reshape(4 * window, DEPTH).astype(jnp.bfloat16)
         scale = jnp.broadcast_to(scale_columns[at, c : c + 1], (DEPTH, LANES)).astype(jnp.float32)
         weights = jnp.concatenate([(scale * cosine[at, :]).astype(jnp.bfloat16), (scale * sine[at, :]).astype(jnp.bfloat16)], axis=1)
         part = jnp.dot(rows, weights, preferred_element_type=jnp.float32)
@@ -219,9 +219,14 @@
         total[...] = jnp.where(part == 0, 0.0, total[...]) + summed
 
     def leave():
-        copy = pltpu.make_async_copy(total, out_hbm.at[:, 0, :], sem)
-        copy.start()
-        copy.wait()
+        sides = [
+            pltpu.make_async_copy(total.at[:, at], out_hbm.at[:, 0, at], sem.at[k])
+            for k, at in enumerate((slice(0, LANES), slice(LANES, 2 * LANES)))
+        ]
+        for copy in sides:
+            copy.start()
+        for copy in sides:
+            copy.wait()
 
     if parts == 1:
         leave()
@@ -246,7 +251,7 @@
         out_shape=jax.ShapeDtypeStruct((trials, 1, 2 * LANES), jnp.float32),
         scratch_shapes=[
             pltpu.VMEM((trials, 2 * LANES), jnp.float32),
-            pltpu.SemaphoreType.DMA(()),
+            pltpu.SemaphoreType.DMA((2,)),
         ],
         compiler_params=pltpu.CompilerParams(vmem_limit_bytes=VMEM_LIMIT),
         name="dedisperse",

time: 23.9 us -> 23.9 us (level)
  no operation moved by 1% of the time
where the time goes in v7:
time: 23.9 us; the launch traced here: 23.6 us
  blocking collectives  17.2 us (72%)
  Pallas kernels  6.38 us (27%)
    all_to_all x1, blocking collectives, local(): lax.all_to_all(outgoing, 'chan', split_axis=0, concat_axis=0, tiled=True)  17.2 us
    pallas_call x1, Pallas kernels, beams(): pl.pallas_call(functools.partial(beam_kernel, chan_total, blocks, divisor...  4.88 us
    pallas_call x1, Pallas kernels, dedisperse(): pl.pallas_call(functools.partial(dedisperse_kernel, scaling, sources // g...  1.5 us

profile of v7, /device:TPU:0, one launch (start us, length us, event | category | flops | bytes accessed | tf_op | source)
XLA Modules:
  0.0 23.6 jit_solution(17113852565704691085)
XLA Ops:
  0.0 4.9 %beams.1 = (bf16[2,8,64,128]{3,2,1,0:T(8,128)(2,1)S(1)}, f32[256,256]{1,0:T(8,128)S(1)}) custom-call(s32[16,2,2,32,1024]{4,3,2,1,0:T(8,128)} %volt_hbm.1, s32[16,1024]{1,0:T(8,128)} %scales_hbm.1, f32[3,1024]{1,0:T(4,128)} %pos_hbm.1, f32[3,128]{1,0:T(4,128)} %dirs_hbm.1, s32[1,256]{1,0:T(1,128)} %bitcast.3), custom_call_target="tpu_custom_call" | custom-call | tf_op jit(solution)/shard_map/beams/pallas_call | solution.py:168
  4.9 17.2 %all_to_all.5.arrived_ref = bf16[16,64,128]{2,1,0:T(8,128)(2,1)S(1)} all-to-all(bf16[16,64,128]{2,1,0:T(8,128)(2,1)S(1)} %bitcast.2), channel_id=1, replica_groups=mesh['grp'=2,'chan'=16] {'chan'}, dimensions={0} | all-to-all | bytes 524288 | tf_op jit(solution)/shard_map/all_to_all | solution.py:266
  22.1 1.5 %dedisperse.1 = f32[256,1,256]{2,1,0:T(1,128)} custom-call(bf16[16,64,128]{2,1,0:T(8,128)(2,1)S(1)} %all_to_all.5.arrived_ref, f32[256,256]{1,0:T(8,128)S(1)} %get-tuple-element.8.delays_ref), custom_call_target="tpu_custom_call" | custom-call | tf_op jit(solution)/shard_map/dedisperse/pallas_call | solution.py:243
